TPU v7x, 32 devices: a whole 2x2x4 slice. The times are simulated.
32 devices in a mesh: seq: 8 (over z, x), rep: 4 (over y, core).
Axes of the slice: x: 2, y: 2, z: 4, core: 2. Of those that a mesh axis runs over, the one named last changes fastest.
Arguments:
- tokens: bfloat16 [4, 2048, 1024], P('rep', 'seq'), may hold values from -6 to 6
- cotangent: bfloat16 [4, 2048, 1024], P('rep', 'seq'), may hold values from -6 to 6
- segment_ids: int32 [4, 2048], P('rep', 'seq'), may hold values from -1 to 2, as said below
- input_gain: bfloat16 [1024], P(('seq', 'rep')), may hold values from 0.5 to 1.5
- ssm_input: bfloat16 [1024, 3072], P(('seq', 'rep')), may hold values from -0.1875 to 0.1875
- state_proj: bfloat16 [1024, 256], P(('seq', 'rep')), may hold values from -0.02734375 to 0.02734375
- step_proj: bfloat16 [1024, 24], P(('seq', 'rep')), may hold values from -0.1875 to 0.1875
- ssm_output: bfloat16 [1024, 1536], P(('seq', 'rep')), may hold values from -0.0390625 to 0.0390625
- qkv_proj: bfloat16 [1024, 768], P(('seq', 'rep')), may hold values from -0.1875 to 0.1875
- attn_output: bfloat16 [1024, 512], P(('seq', 'rep')), may hold values from -3 to 3
- ffn_gain: bfloat16 [1024], P(('seq', 'rep')), may hold values from 0.5 to 1.5
- gate_up: bfloat16 [1024, 4096], P(('seq', 'rep')), may hold values from -0.1875 to 0.1875
- down_proj: bfloat16 [1024, 2048], P(('seq', 'rep')), may hold values from -0.125 to 0.125
- head_params: float32 [3, 24], replicated, may hold values from -13 to 2, as said below
Outputs:
- layer_out: bfloat16 [4, 2048, 1024], P('rep', 'seq')
- input_grad: bfloat16 [4, 2048, 1024], P('rep', 'seq')
- input_gain_grad: float32 [1024], P(('seq', 'rep'))
- ssm_input_grad: float32 [1024, 3072], P(('seq', 'rep'))
- state_proj_grad: float32 [1024, 256], P(('seq', 'rep'))
- step_proj_grad: float32 [1024, 24], P(('seq', 'rep'))
- ssm_output_grad: float32 [1024, 1536], P(('seq', 'rep'))
- qkv_proj_grad: float32 [1024, 768], P(('seq', 'rep'))
- attn_output_grad: float32 [1024, 512], P(('seq', 'rep'))
- ffn_gain_grad: float32 [1024], P(('seq', 'rep'))
- gate_up_grad: float32 [1024, 4096], P(('seq', 'rep'))
- down_proj_grad: float32 [1024, 2048], P(('seq', 'rep'))
- head_params_grad: float32 [3, 24], replicated
Inputs may be any that keep to these rules, and one draw needn't show every extreme that they name: `segment_ids`: per group, live rows carry a sequence number 0, 1 or 2 and padding rows -1. Rows form blocks of 32; a device's 8 slots hold 6 to 8 used blocks first, the rest padding; the last device of seq and one other use all 8. Each sequence fills a run of consecutive used blocks in row order and is live on a leading part of its last block. Sequence 1 has live rows on the first and on the last device of seq. `head_params`: row 0 holds logarithms of decay rates, row 1 step biases, row 2 skip weights.
All inputs are finite; a program needn't handle non-finite values.
Results may differ from a plain program's by a relative error of at most 0.014.
Values may be sent and summed in bfloat16 or wider, within the bound.
A program may use at most 256 MiB of HBM per device.

v0:
```python
from functools import partial
import math

import jax
import jax.numpy as jnp
from jax import lax
from jax.sharding import PartitionSpec as P

FF = 2048
HEADS = 8
KV_HEADS = 2
HEAD_DIM = 64
SSM_HEADS = 24
SSM_DIM = 64
STATE = 128
BLOCK = 32
D_SSM = 1536


EPS = 1e-06
WILD = -3.0
HIGH = lax.Precision.HIGHEST


def carried_in(x, axis, join, neutral):
    place = lax.axis_index(axis)
    gathered = jax.tree.map(
        lambda a, kind: lax.all_gather(a.astype(kind), axis),
        x,
        (jnp.bfloat16, jnp.bfloat16, jnp.bfloat16, jnp.bfloat16),
    )
    state = jax.tree.map(lambda a, e: jnp.zeros_like(a) + jnp.asarray(e, a.dtype), x, neutral)

    def carried_one(turn, state):
        return join(
            state,
            jax.tree.map(
                lambda a, own: lax.dynamic_index_in_dim(a, turn, 0, False).astype(own.dtype),
                gathered,
                x,
            ),
        )

    return lax.fori_loop(0, place, carried_one, state)


def entering(x, axis, join, neutral):
    count = lax.axis_size(axis)
    place = lax.axis_index(axis)
    ahead = count - 1 - place
    gathered = jax.tree.map(
        lambda a, kind: lax.all_gather(a.astype(kind), axis),
        x,
        jax.tree.map(lambda a: jnp.bfloat16 if a.dtype == jnp.float32 else a.dtype, x),
    )
    state = jax.tree.map(lambda a, e: jnp.zeros_like(a) + jnp.asarray(e, a.dtype), x, neutral)

    def entering_one(turn, state):
        source = count - 1 - turn
        return join(
            state,
            jax.tree.map(
                lambda a, own: lax.dynamic_index_in_dim(a, source, 0, False).astype(own.dtype),
                gathered,
                x,
            ),
        )

    return lax.fori_loop(0, ahead, entering_one, state)


def project(left, right):
    return jnp.dot(left, right, preferred_element_type=jnp.float32)


def project_back(left, right):
    return lax.dot_general(
        left, right, (((1,), (1,)), ((), ())), preferred_element_type=jnp.float32
    )


def outer_sum(left, right):
    return lax.dot_general(
        left, right, (((0,), (0,)), ((), ())), preferred_element_type=jnp.float32
    )


def norm_rows(values, gain):
    inverse = lax.rsqrt(jnp.mean(values * values, axis=-1, keepdims=True) + EPS)
    return (values * inverse * gain, inverse)


def norm_back(grad, values, inverse, gain):
    scaled = values * inverse
    gain_grad = jnp.sum(grad * scaled, axis=0)
    weighted = grad * gain
    return (
        inverse * (weighted - scaled * jnp.mean(weighted * scaled, axis=-1, keepdims=True)),
        gain_grad,
    )


def stretch_math(state, signal, entry_map, read_map, step_size, log_decay, restarts):
    length = signal.shape[0]
    cumul = jnp.cumsum(log_decay, axis=0)
    counter = jnp.cumsum(restarts, axis=0)
    places = jnp.arange(length)
    joined = (counter[:, None] == counter[None, :]) & (places[None, :] <= places[:, None])
    spread = cumul.T[:, :, None] - cumul.T[:, None, :]
    decay = jnp.where(joined[None], jnp.exp(jnp.where(joined[None], spread, 0.0)), 0.0)
    intersection = jnp.dot(read_map, entry_map.T, precision=HIGH)
    mixing = decay * intersection[None] * step_size.T[:, None, :]
    within = jnp.einsum("hts,shp->thp", mixing, signal, precision=HIGH)
    opening = jnp.where((counter == 0)[:, None], jnp.exp(cumul), 0.0)
    carried = jnp.einsum("tn,hpn->thp", read_map, state, precision=HIGH) * opening[:, :, None]
    closing = jnp.where((counter == counter[-1])[:, None], jnp.exp(cumul[-1][None, :] - cumul), 0.0)
    scaled = signal * (closing * step_size)[:, :, None]
    renewed = opening[-1][:, None, None] * state + jnp.einsum(
        "shp,sn->hpn", scaled, entry_map, precision=HIGH
    )
    return (within + carried, renewed, opening)


def local_ssm(signal, states, step_raw, head_params, restarts):
    rows = signal.shape[0]
    step_size = jax.nn.softplus(step_raw + head_params[1])
    log_decay = -step_size * jnp.exp(head_params[0])
    count = rows // BLOCK
    pieces = (
        signal.reshape(count, BLOCK, SSM_HEADS, SSM_DIM),
        states[:, :STATE].reshape(count, BLOCK, STATE),
        states[:, STATE:].reshape(count, BLOCK, STATE),
        step_size.reshape(count, BLOCK, SSM_HEADS),
        log_decay.reshape(count, BLOCK, SSM_HEADS),
        restarts.reshape(count, BLOCK),
    )

    def advance(carry, piece):
        state, prefix = carry
        part, renewed, opening = stretch_math(state, *piece)
        return ((renewed, prefix * opening[-1]), (part, prefix[None, :] * opening))

    start = (
        jnp.zeros((SSM_HEADS, SSM_DIM, STATE), jnp.float32),
        jnp.ones((SSM_HEADS,), jnp.float32),
    )
    (ending, decay), (parts, reach) = lax.scan(advance, start, pieces)
    mixed = parts.reshape(rows, SSM_HEADS, SSM_DIM) + head_params[2][None, :, None] * signal
    return (mixed, ending, decay, reach.reshape(rows, SSM_HEADS))


def add_carry(states, reach, entry):
    return reach[:, :, None] * jnp.einsum("tn,hpn->thp", states[:, STATE:], entry, precision=HIGH)


def link_states(early, late):
    decay_e, state_e, first_e, last_e = early
    decay_l, state_l, first_l, last_l = late
    joined = (last_e == first_l) | (last_e == WILD) | (first_l == WILD)
    keep = jnp.where(joined, 1.0, 0.0)
    return (
        decay_e * decay_l * keep,
        state_l + (decay_l * keep)[:, None, None] * state_e,
        jnp.where(first_e == WILD, first_l, first_e),
        jnp.where(last_l == WILD, last_e, last_l),
    )


def link_grads(early, late):
    factor_e, grad_e = early
    factor_l, grad_l = late
    return (factor_l * factor_e, grad_l + factor_l[:, None, None] * grad_e)


def visible(seg_float, seg_piece, query_pos, start, span):
    key_pos = start + jnp.arange(span)
    same = seg_float[:, None] == seg_piece.astype(jnp.float32)[None, :]
    causal = key_pos[None, :] <= query_pos[:, None]
    return (same & causal)[:, None, None, :]


def body(
    tokens,
    cotangent,
    segment_ids,
    input_gain,
    ssm_input,
    state_proj,
    step_proj,
    ssm_output,
    qkv_proj,
    attn_output,
    ffn_gain,
    gate_up,
    down_proj,
    head_params,
):
    rows = tokens.shape[1]
    width = HEADS * HEAD_DIM
    kv_width = KV_HEADS * HEAD_DIM
    group = HEADS // KV_HEADS
    scale = HEAD_DIM ** (-0.5)
    shards = (
        input_gain,
        ssm_input,
        state_proj,
        step_proj,
        ssm_output,
        qkv_proj,
        attn_output,
        ffn_gain,
        gate_up,
        down_proj,
    )
    (
        gain_first,
        inner_full,
        states_full,
        step_full,
        mixer_full,
        project_full,
        attend_full,
        gain_second,
        gate_full,
        down_full,
    ) = (
        lax.all_gather(shards[0], ("seq", "rep"), axis=0, tiled=True),
        lax.all_gather(shards[1], ("seq", "rep"), axis=0, tiled=True),
        lax.all_gather(shards[2], ("seq", "rep"), axis=0, tiled=True),
        lax.all_gather(shards[3], ("seq", "rep"), axis=0, tiled=True),
        lax.all_gather(shards[4], ("seq", "rep"), axis=0, tiled=True),
        lax.all_gather(shards[5], ("seq", "rep"), axis=0, tiled=True),
        lax.all_gather(shards[6], ("seq", "rep"), axis=0, tiled=True),
        lax.all_gather(shards[7], ("seq", "rep"), axis=0, tiled=True),
        lax.all_gather(shards[8], ("seq", "rep"), axis=0, tiled=True),
        lax.all_gather(shards[9], ("seq", "rep"), axis=0, tiled=True),
    )
    resident = tokens[0].astype(jnp.float32)
    segments = segment_ids[0]
    live = jnp.where(segments >= 0, 1.0, 0.0)[:, None]
    first_gain = gain_first.astype(jnp.float32)
    normed_float, inverse_one = norm_rows(resident, first_gain)
    normed = normed_float.astype(jnp.bfloat16)
    inner = project(normed, inner_full).astype(jnp.bfloat16)
    states = project(normed, states_full).astype(jnp.bfloat16)
    step_raw = project(normed, step_full)
    projected = project(normed, project_full).astype(jnp.bfloat16)
    signal = inner[:, D_SSM:].astype(jnp.float32).reshape(rows, SSM_HEADS, SSM_DIM)
    gate_float = inner[:, :D_SSM].astype(jnp.float32).reshape(rows, SSM_HEADS, SSM_DIM)
    states_float = states.astype(jnp.float32)
    earlier = jnp.concatenate([segments[:1], segments[:-1]])
    restarts = jnp.where(segments != earlier, 1.0, 0.0)
    (mixed_zero, ending, decay, reach), pull_local = jax.vjp(
        partial(local_ssm, restarts=restarts), signal, states_float, step_raw, head_params
    )
    opening_seg = segments[0].astype(jnp.float32)
    closing_seg = segments[-1].astype(jnp.float32)
    prefix = carried_in(
        (decay, ending, opening_seg, closing_seg),
        "seq",
        link_states,
        (jnp.ones_like(decay), jnp.zeros_like(ending), jnp.float32(WILD), jnp.float32(WILD)),
    )
    matched = jnp.where((prefix[3] == opening_seg) | (prefix[3] == WILD), 1.0, 0.0)
    entry = matched * prefix[1]
    carry_term, pull_carry = jax.vjp(add_carry, states_float, reach, entry)
    mixed = mixed_zero + carry_term
    sig_gate = jax.nn.sigmoid(gate_float)
    gated = (mixed * gate_float * sig_gate).reshape(rows, D_SSM).astype(jnp.bfloat16)
    queries = projected[:, :width].reshape(rows, KV_HEADS, group, HEAD_DIM)
    key_vals = projected[:, width:]
    seg_wire = segments.astype(jnp.bfloat16)
    seg_float = segments.astype(jnp.float32)
    row_start = lax.axis_index("seq") * rows
    query_pos = row_start + jnp.arange(rows)
    row_last = row_start + rows - 1
    initial = (
        jnp.full((rows, KV_HEADS, group), -1e30, jnp.float32),
        jnp.zeros((rows, KV_HEADS, group), jnp.float32),
        jnp.zeros((rows, KV_HEADS, group, HEAD_DIM), jnp.float32),
    )
    start = jnp.int32(0)
    kv_piece = lax.all_gather(key_vals, "seq", axis=0, tiled=True)
    seg_piece = lax.all_gather(seg_wire, "seq", axis=0, tiled=True)
    span = kv_piece.shape[0]

    def absorb_work(current):
        top, total, weighted = current
        keys = kv_piece[:, :kv_width].reshape(span, KV_HEADS, HEAD_DIM)
        values = kv_piece[:, kv_width:].reshape(span, KV_HEADS, HEAD_DIM).astype(jnp.float32)
        scores = (
            jnp.einsum("tgjd,sgd->tgjs", queries, keys, preferred_element_type=jnp.float32) * scale
        )
        allowed = visible(seg_float, seg_piece, query_pos, start, span)
        masked = jnp.where(allowed, scores, -1e30)
        new_top = jnp.maximum(top, jnp.max(masked, axis=-1))
        probability = jnp.where(allowed, jnp.exp(masked - new_top[..., None]), 0.0)
        total = jnp.sum(probability, axis=-1)
        weighted = jnp.einsum("tgjs,sgd->tgjd", probability, values, precision=HIGH)
        return (new_top, total, weighted)

    def unchanged(current):
        return current

    top, total, weighted = lax.cond(start <= row_last, absorb_work, unchanged, initial)
    attended_float = weighted / total[..., None]
    log_total = top + jnp.log(total)
    attended = attended_float.reshape(rows, width).astype(jnp.bfloat16)
    mixed_out = project_back(gated, mixer_full) + project_back(attended, attend_full)
    hidden = resident + live * mixed_out
    second_gain = gain_second.astype(jnp.float32)
    normed2_float, inverse_two = norm_rows(hidden, second_gain)
    normed2 = normed2_float.astype(jnp.bfloat16)
    gate_vals = project(normed2, gate_full)
    gate_part = gate_vals[:, :FF]
    up_part = gate_vals[:, FF:]
    sigma = jax.nn.sigmoid(gate_part)
    activated = (gate_part * sigma * up_part).astype(jnp.bfloat16)
    result = hidden + live * project_back(activated, down_full)
    layer_out = result.astype(jnp.bfloat16)[None]
    upstream = cotangent[0].astype(jnp.float32)
    ffn_wire = (live * upstream).astype(jnp.bfloat16)
    down_grad = outer_sum(ffn_wire, activated)
    activated_grad = project(ffn_wire, down_full)
    gate_grad = activated_grad * up_part * sigma * (1.0 + gate_part * (1.0 - sigma))
    up_grad = activated_grad * gate_part * sigma
    gate_up_wire = jnp.concatenate([gate_grad, up_grad], axis=1).astype(jnp.bfloat16)
    gate_up_grad = outer_sum(normed2, gate_up_wire)
    normed2_grad = project_back(gate_up_wire, gate_full)
    hidden_back, gain_two_grad = norm_back(normed2_grad, hidden, inverse_two, second_gain)
    hidden_grad = upstream + hidden_back
    mixed_wire = (live * hidden_grad).astype(jnp.bfloat16)
    mixer_out_grad = outer_sum(mixed_wire, gated)
    attend_out_grad = outer_sum(mixed_wire, attended)
    gated_wire = project(mixed_wire, mixer_full).astype(jnp.bfloat16)
    attended_wire = project(mixed_wire, attend_full).astype(jnp.bfloat16)
    gated_grad = gated_wire.astype(jnp.float32).reshape(rows, SSM_HEADS, SSM_DIM)
    mixed_grad = gated_grad * gate_float * sig_gate
    gate_float_grad = gated_grad * mixed * sig_gate * (1.0 + gate_float * (1.0 - sig_gate))
    states_grad_carry, reach_grad, entry_grad = pull_carry(mixed_grad)
    later = entering(
        (matched * decay, matched * entry_grad),
        "seq",
        link_grads,
        (jnp.ones_like(decay), jnp.zeros_like(entry_grad)),
    )
    end_grad = later[1]
    decay_grad = jnp.sum(end_grad * entry, axis=(1, 2))
    signal_grad, states_grad_local, step_grad, head_grad = pull_local(
        (mixed_grad, end_grad, decay_grad, reach_grad)
    )
    inner_wire = jnp.concatenate(
        [gate_float_grad.reshape(rows, D_SSM), signal_grad.reshape(rows, D_SSM)], axis=1
    ).astype(jnp.bfloat16)
    states_wire = (states_grad_carry + states_grad_local).astype(jnp.bfloat16)
    step_wire = step_grad.astype(jnp.bfloat16)
    out_grad = attended_wire.reshape(rows, KV_HEADS, group, HEAD_DIM)
    out_grad_float = out_grad.astype(jnp.float32)
    delta = jnp.sum(out_grad_float * attended_float, axis=-1)
    kv_all, seg_all = (
        lax.all_gather(key_vals, "seq", axis=0, tiled=True),
        lax.all_gather(seg_wire, "seq", axis=0, tiled=True),
    )
    group_rows = kv_all.shape[0]
    block = math.gcd(group_rows, 512)
    count = group_rows // block

    def key_block(query_sum, piece):
        kv_piece, seg_piece, start = piece

        def key_work(unused):
            keys = kv_piece[:, :kv_width].reshape(block, KV_HEADS, HEAD_DIM)
            values = kv_piece[:, kv_width:].reshape(block, KV_HEADS, HEAD_DIM)
            scores = (
                jnp.einsum("tgjd,sgd->tgjs", queries, keys, preferred_element_type=jnp.float32)
                * scale
            )
            allowed = visible(seg_float, seg_piece, query_pos, start, block)
            probability = jnp.where(
                allowed, jnp.exp(jnp.where(allowed, scores - log_total[..., None], -1e30)), 0.0
            )
            values_grad = jnp.einsum("tgjs,tgjd->sgd", probability, out_grad_float, precision=HIGH)
            prob_grad = jnp.einsum(
                "tgjd,sgd->tgjs", out_grad, values, preferred_element_type=jnp.float32
            )
            score_wire = (probability * (prob_grad - delta[..., None])).astype(jnp.bfloat16)
            query_part = (
                jnp.einsum("tgjs,sgd->tgjd", score_wire, keys, preferred_element_type=jnp.float32)
                * scale
            )
            keys_grad = (
                jnp.einsum(
                    "tgjs,tgjd->sgd", score_wire, queries, preferred_element_type=jnp.float32
                )
                * scale
            )
            block_grad = jnp.concatenate(
                [keys_grad.reshape(block, kv_width), values_grad.reshape(block, kv_width)], axis=1
            )
            return (query_part, block_grad)

        def skip(unused):
            return (jnp.zeros_like(query_sum), jnp.zeros((block, 2 * kv_width), jnp.float32))

        query_part, block_grad = lax.cond(start <= row_last, key_work, skip, 0)
        return (query_sum + query_part, block_grad)

    starts = jnp.arange(count) * block
    query_grad, key_grads = lax.scan(
        key_block,
        jnp.zeros((rows, KV_HEADS, group, HEAD_DIM), jnp.float32),
        (kv_all.reshape(count, block, 2 * kv_width), seg_all.reshape(count, block), starts),
    )
    own_kv = lax.psum_scatter(
        key_grads.reshape(group_rows, 2 * kv_width).astype(jnp.bfloat16),
        "seq",
        scatter_dimension=0,
        tiled=True,
    ).astype(jnp.float32)
    projected_wire = jnp.concatenate([query_grad.reshape(rows, width), own_kv], axis=1).astype(
        jnp.bfloat16
    )
    inner_grad = outer_sum(normed, inner_wire)
    states_grad = outer_sum(normed, states_wire)
    step_weight_grad = outer_sum(normed, step_wire)
    project_grad = outer_sum(normed, projected_wire)
    normed_grad = (
        project_back(inner_wire, inner_full)
        + project_back(states_wire, states_full)
        + project_back(step_wire, step_full)
        + project_back(projected_wire, project_full)
    )
    resident_back, gain_one_grad = norm_back(normed_grad, resident, inverse_one, first_gain)
    input_grad = (hidden_grad + resident_back).astype(jnp.bfloat16)[None]
    head_sum = lax.psum(head_grad, ("seq", "rep"))
    owned = (
        lax.psum_scatter(gain_one_grad, ("seq", "rep"), scatter_dimension=0, tiled=True),
        lax.psum_scatter(inner_grad, ("seq", "rep"), scatter_dimension=0, tiled=True),
        lax.psum_scatter(states_grad, ("seq", "rep"), scatter_dimension=0, tiled=True),
        lax.psum_scatter(step_weight_grad, ("seq", "rep"), scatter_dimension=0, tiled=True),
        lax.psum_scatter(mixer_out_grad, ("seq", "rep"), scatter_dimension=0, tiled=True),
        lax.psum_scatter(project_grad, ("seq", "rep"), scatter_dimension=0, tiled=True),
        lax.psum_scatter(attend_out_grad, ("seq", "rep"), scatter_dimension=0, tiled=True),
        lax.psum_scatter(gain_two_grad, ("seq", "rep"), scatter_dimension=0, tiled=True),
        lax.psum_scatter(gate_up_grad, ("seq", "rep"), scatter_dimension=0, tiled=True),
        lax.psum_scatter(down_grad, ("seq", "rep"), scatter_dimension=0, tiled=True),
    )
    return (
        layer_out,
        input_grad,
        owned[0],
        owned[1],
        owned[2],
        owned[3],
        owned[4],
        owned[5],
        owned[6],
        owned[7],
        owned[8],
        owned[9],
        head_sum,
    )


def solution(mesh):
    placed = (
        P("rep", "seq", None),
        P("rep", "seq", None),
        P("rep", "seq"),
        P(("seq", "rep")),
        P(("seq", "rep"), None),
        P(("seq", "rep"), None),
        P(("seq", "rep"), None),
        P(("seq", "rep"), None),
        P(("seq", "rep"), None),
        P(("seq", "rep"), None),
        P(("seq", "rep")),
        P(("seq", "rep"), None),
        P(("seq", "rep"), None),
        P(),
    )
    return jax.shard_map(
        body,
        mesh=mesh,
        in_specs=placed,
        out_specs=(
            P("rep", "seq", None),
            P("rep", "seq", None),
            P(("seq", "rep")),
            P(("seq", "rep"), None),
            P(("seq", "rep"), None),
            P(("seq", "rep"), None),
            P(("seq", "rep"), None),
            P(("seq", "rep"), None),
            P(("seq", "rep"), None),
            P(("seq", "rep")),
            P(("seq", "rep"), None),
            P(("seq", "rep"), None),
            P(),
        ),
        check_vma=False,
    )
```

profile of v0, /device:TPU:9, one launch (start us, length us, event | category | flops | bytes accessed | tf_op | source)
XLA Modules:
  0.0 2220.5 jit_solution(14680315902981982678)
XLA Ops:
  10.7 39.9 %all-reduce.18 = (bf16[1024]{0:T(1024)(128)(2,1)S(1)}, bf16[1024]{0:T(1024)(128)(2,1)S(1)}) all-reduce(bf16[1024]{0:T(1024)(128)(2,1)S(1)} %dynamic-update-slice, bf16[1024]{0:T(1024)(128)(2,1)S(1)} %dynamic-update-slice.4), channel_id=1, replica_groups=mesh['seq'=8,'rep'=4] {'seq','rep'}, use_global_device_ids=true, to_apply=%add.9 | all-reduce | flops 2048 | bytes 8192
  55.4 35.8 %all-gather.6 = bf16[32,32,24]{1,2,0:T(8,128)(2,1)S(1)} all-gather(bf16[1,32,24]{1,2,0:T(8,128)(2,1)} %bitcast.696), channel_id=1, replica_groups=mesh['seq'=8,'rep'=4] {'seq','rep'}, dimensions={0}, use_global_device_ids=true | all-gather | bytes 50688 | tf_op jit(solution)/shard_map/all_gather | solution.py:230
  95.7 39.7 %all_gather.77 = bf16[1024,256]{1,0:T(8,128)(2,1)S(1)} all-gather(bf16[32,256]{1,0:T(8,128)(2,1)} %param.33), channel_id=1, replica_groups=mesh['seq'=8,'rep'=4] {'seq','rep'}, dimensions={0}, use_global_device_ids=true | all-gather | bytes 540672 | tf_op jit(solution)/shard_map/all_gather | solution.py:229
  156.8 202.7 %while.139 = (s32[]{:T(128)}, f32[24,64,128]{2,1,0:T(8,128)S(1)}, f32[24]{0:T(128)S(1)}, f32[8,32,24,64]{3,2,1,0:T(8,128)}, f32[8,32,24]{2,1,0:T(8,128)S(1)}, /*...) while((s32[]{:T(128)}, f32[24,64,128]{2,1,0:T(8,128)S(1)}, ...), condition=%wide.region_4.5_spmd.clone, body=%wide.region_1.4_spmd.clone.sunk | while | flops 172904784 | bytes 9533568 | solution.py:147
  367.3 15.9 all-gather.3
  383.4 24.9 %conditional.2 = (f32[256,2,4]{0,2,1:T(4,128)}, f32[256,2,4]{0,2,1:T(4,128)}, f32[256,2,4,64]{0,3,2,1:T(8,128)}, f32[256,2,4]{0,2,1:T(4,128)S(1)}) conditional(s32[]{:T(128)} %convert_element_type.233, () %tuple.105, (f32[256]{0:T(256)S(1)}, bf16[1,2048]{1,0:T(2,128)(2,1)S(1)}, s32[]{:T(128)}, bf16[2048,256]{1,0:T(8,128)(2,1)}, ...), branch_computations={%region_7.8_spmd, %region_8.11_spmd} | conditional | flops 3810001152 | bytes 58556456 | solution.py:305
  417.7 15.7 all-reduce.19
  449.1 34.0 %all-gather.19.cloned.1.call-done = bf16[1024,1536]{1,0:T(8,128)(2,1)} async-done(((bf16[32,1536]{1,0:T(8,128)(2,1)}), bf16[1024,1536]{1,0:T(8,128)(2,1)}) %all-gather.19.cloned.1.call-update) | async-done | bytes 3145744 | tf_op jit(solution)/shard_map/all_gather | solution.py:231
  487.0 51.6 %all-gather.25.cloned.1.call-done = bf16[1024,512]{1,0:T(8,128)(2,1)} async-done(((bf16[32,512]{1,0:T(8,128)(2,1)}), bf16[1024,512]{1,0:T(8,128)(2,1)}) %all-gather.25.cloned.1.call-update) | async-done | bytes 1048592 | tf_op jit(solution)/shard_map/all_gather | solution.py:233
  540.8 78.0 %all-gather.27.cloned.1.call-done = bf16[1024,4096]{1,0:T(8,128)(2,1)} async-done(((bf16[32,4096]{1,0:T(8,128)(2,1)}), bf16[1024,4096]{1,0:T(8,128)(2,1)}) %all-gather.27.cloned.1.call-update) | async-done | bytes 8388624 | tf_op jit(solution)/shard_map/all_gather | solution.py:235
  626.5 55.7 %all-gather.29.cloned.1.call-done = bf16[1024,2048]{1,0:T(8,128)(2,1)} async-done(((bf16[32,2048]{1,0:T(8,128)(2,1)}), bf16[1024,2048]{1,0:T(8,128)(2,1)}) %all-gather.29.cloned.1.call-update) | async-done | bytes 4194320 | tf_op jit(solution)/shard_map/all_gather | solution.py:236
  712.7 14.2 all-reduce.14
  736.5 32.6 %while.140 = (s32[]{:T(128)}, f32[256,2,4,64]{0,3,2,1:T(8,128)S(1)}, bf16[4,512,256]{2,1,0:T(8,128)(2,1)}, s32[4]{0:T(128)S(1)}, s32[]{:T(128)}, /*index=5*/f32[...) while((s32[]{:T(128)}, f32[256,2,4,64]{0,3,2,1:T(8,128)S(1)}, ...), condition=%wide.region_33.34_spmd.clone, body=%wide.region_30.33_spmd.clone.sunk | while | flops 1355154688 | bytes 28089180 | solution.py:409
  737.8 11.6 conditional.5
  751.8 11.6 conditional.5
  781.7 283.1 %while.138 = (s32[]{:T(128)}, f32[24,64,128]{2,1,0:T(8,128)S(1)}, f32[24]{0:T(128)}, f32[8,32,24,64]{3,2,1,0:T(8,128)}, f32[8,32,128]{2,1,0:T(8,128)}, /*index=5...) while((s32[]{:T(128)}, f32[24,64,128]{2,1,0:T(8,128)S(1)}, ...), condition=%wide.region_28.29_spmd, body=%wide.region_17.28_spmd.sunk | while | flops 344376832 | bytes 11459905 | solution.py:147
  1135.3 58.1 %all-reduce.17 = (f32[1024]{0:T(1024)S(1)}, f32[1024]{0:T(1024)S(1)}, f32[3,24]{1,0:T(4,128)}) all-reduce(f32[1024]{0:T(1024)S(1)} %get-tuple-element.2209, f32[1024]{0:T(1024)S(1)} %copy-done.66, f32[3,24]{1,0:T(4,128)S(1)} %copy-done.62), channel_id=9, replica_groups=mesh['seq'=8,'rep'=4] {'seq','rep'}, use_global_device_ids=true, to_apply=%region_37.38.clone | all-reduce | flops 2120 | bytes 16960
  1200.5 133.7 %reduce-scatter.22.cloned.1.call-done = f32[32,512]{1,0:T(8,128)} async-done(((f32[1024,512]{1,0:T(8,128)}), f32[32,512]{1,0:T(8,128)}) %reduce-scatter.22.cloned.1.call-update) | async-done | bytes 65552 | tf_op jit(solution)/shard_map/reduce_scatter | solution.py:443
  1334.2 126.7 %reduce-scatter.20.cloned.1.call-done = f32[32,768]{1,0:T(8,128)} async-done(((f32[1024,768]{1,0:T(8,128)}), f32[32,768]{1,0:T(8,128)}) %reduce-scatter.20.cloned.1.call-update) | async-done | bytes 98320 | tf_op jit(solution)/shard_map/reduce_scatter | solution.py:442
  1460.9 114.3 %reduce-scatter.16.cloned.1.call-done = f32[32,256]{1,0:T(8,128)} async-done(((f32[1024,256]{1,0:T(8,128)}), f32[32,256]{1,0:T(8,128)}) %reduce-scatter.16.cloned.1.call-update) | async-done | bytes 32784 | tf_op jit(solution)/shard_map/reduce_scatter | solution.py:439
  1575.2 138.6 %reduce-scatter.18.cloned.1.call-done = f32[32,1536]{1,0:T(8,128)} async-done(((f32[1024,1536]{1,0:T(8,128)}), f32[32,1536]{1,0:T(8,128)}) %reduce-scatter.18.cloned.1.call-update) | async-done | bytes 196624 | tf_op jit(solution)/shard_map/reduce_scatter | solution.py:441
  1713.9 130.3 %reduce-scatter.26.cloned.1.call-done = f32[32,2048]{1,0:T(8,128)} async-done(((f32[1024,2048]{1,0:T(8,128)}), f32[32,2048]{1,0:T(8,128)}) %reduce-scatter.26.cloned.1.call-update) | async-done | bytes 262160 | tf_op jit(solution)/shard_map/reduce_scatter | solution.py:446
  1844.1 179.8 %reduce-scatter.14.cloned.1.call-done = f32[32,3072]{1,0:T(8,128)} async-done(((f32[1024,3072]{1,0:T(8,128)}), f32[32,3072]{1,0:T(8,128)}) %reduce-scatter.14.cloned.1.call-update) | async-done | bytes 393232 | tf_op jit(solution)/shard_map/reduce_scatter | solution.py:438
  2023.9 189.3 %reduce-scatter.24.cloned.1.call-done = f32[32,4096]{1,0:T(8,128)} async-done(((f32[1024,4096]{1,0:T(8,128)}), f32[32,4096]{1,0:T(8,128)}) %reduce-scatter.24.cloned.1.call-update) | async-done | bytes 524304 | tf_op jit(solution)/shard_map/reduce_scatter | solution.py:445
  (1033 shorter events, 758.6 us)
Async XLA Ops:
  7.2 130.0 %all-gather.21.cloned.1.call-start = ((), (), s32[]{:S(2)}) async-start(), calls=%async_computation.11 | async-start | bytes 1622016 | tf_op jit(solution)/shard_map/all_gather | solution.py:232
  7.9 133.3 %all-gather.17.cloned.1.call-start = ((), (), s32[]{:S(2)}) async-start(), calls=%async_computation.9 | async-start | bytes 6488064 | tf_op jit(solution)/shard_map/all_gather | solution.py:228
  8.7 374.7 %all-gather.23.cloned.1.call-start = ((), (), s32[]{:S(2)}) async-start(), calls=%async_computation.12 | async-start | bytes 1179648 | tf_op jit(solution)/shard_map/all_gather | solution.py:283
  93.5 350.5 %copy-start.64 = (f32[24]{0:T(128)}, f32[24]{0:T(128)S(1)}, u32[]{:S(2)}) copy-start(f32[24]{0:T(128)S(1)} %get-tuple-element.2484) | copy-start | bytes 292
  140.0 293.5 %all-gather.31.cloned.1.call-start = ((), (), s32[]{:S(2)}) async-start(), calls=%async_computation.24 | async-start | bytes 3538944 | tf_op jit(solution)/shard_map/all_gather | solution.py:28
  156.8 226.4 %copy-start.59 = (s32[1,256]{1,0:T(1,128)S(1)}, s32[1,256]{1,0:T(1,128)}, u32[]{:S(2)}) copy-start(s32[1,256]{1,0:T(1,128)} %param.30) | copy-start | bytes 3076
  360.3 122.8 %all-gather.19.cloned.1.call-start = ((), (), s32[]{:S(2)}) async-start(), calls=%async_computation.10 | async-start | bytes 3244032 | tf_op jit(solution)/shard_map/all_gather | solution.py:231
  360.9 177.7 %all-gather.25.cloned.1.call-start = ((), (), s32[]{:S(2)}) async-start(), calls=%async_computation.13 | async-start | bytes 1081344 | tf_op jit(solution)/shard_map/all_gather | solution.py:233
  361.5 257.3 %all-gather.27.cloned.1.call-start = ((), (), s32[]{:S(2)}) async-start(), calls=%async_computation.14 | async-start | bytes 8650752 | tf_op jit(solution)/shard_map/all_gather | solution.py:235
  362.2 320.0 %all-gather.29.cloned.1.call-start = ((), (), s32[]{:S(2)}) async-start(), calls=%async_computation.15 | async-start | bytes 4325376 | tf_op jit(solution)/shard_map/all_gather | solution.py:236
  363.0 406.3 %all-gather.33.cloned.1.call-start = ((), (), s32[]{:S(2)}) async-start(), calls=%async_computation.25 | async-start | bytes 3538944 | tf_op jit(solution)/shard_map/all_gather | solution.py:52
  383.2 310.1 %copy-start.56 = (f32[1,256]{1,0:T(1,128)}, f32[1,256]{1,0:T(1,128)S(1)}, u32[]{:S(2)}) copy-start(f32[1,256]{1,0:T(1,128)S(1)} %compare_select_fusion.4) | copy-start | bytes 3076
  414.2 291.9 %copy-start.46 = (f32[256,24]{0,1:T(8,128)}, f32[256,24]{0,1:T(8,128)S(1)}, u32[]{:S(2)}) copy-start(f32[256,24]{0,1:T(8,128)S(1)} %copy.192) | copy-start | bytes 73732
  709.4 364.4 %reduce-scatter.12.cloned.1.call-start = ((), (), s32[]{:S(2)}) async-start(), calls=%async_computation.16 | async-start | bytes 1179648 | tf_op jit(solution)/shard_map/reduce_scatter | solution.py:414
  769.2 429.9 %reduce-scatter.28.cloned.1.call-start = ((), (), s32[]{:S(2)}) async-start(), calls=%async_computation.26 | async-start | bytes 540672
  781.7 286.5 %copy-start.44 = (f32[1024]{0:T(1024)S(1)}, f32[1024]{0:T(1024)}, u32[]{:S(2)}) copy-start(f32[1024]{0:T(1024)} %copy-done.43) | copy-start | bytes 12292
  781.7 286.5 %copy-start.54 = (f32[256]{0:T(256)S(1)}, f32[256]{0:T(256)}, u32[]{:S(2)}) copy-start(f32[256]{0:T(256)} %copy-done.53) | copy-start | bytes 3076
  1070.6 263.6 %reduce-scatter.22.cloned.1.call-start = ((), (), s32[]{:S(2)}) async-start(), calls=%async_computation.21 | async-start | bytes 2162688 | tf_op jit(solution)/shard_map/reduce_scatter | solution.py:443
  1073.7 387.2 %reduce-scatter.20.cloned.1.call-start = ((), (), s32[]{:S(2)}) async-start(), calls=%async_computation.20 | async-start | bytes 3244032 | tf_op jit(solution)/shard_map/reduce_scatter | solution.py:442
  1077.4 497.8 %reduce-scatter.16.cloned.1.call-start = ((), (), s32[]{:S(2)}) async-start(), calls=%async_computation.18 | async-start | bytes 1081344 | tf_op jit(solution)/shard_map/reduce_scatter | solution.py:439
  1083.2 630.6 %reduce-scatter.18.cloned.1.call-start = ((), (), s32[]{:S(2)}) async-start(), calls=%async_computation.19 | async-start | bytes 6488064 | tf_op jit(solution)/shard_map/reduce_scatter | solution.py:441
  1087.1 757.1 %reduce-scatter.26.cloned.1.call-start = ((), (), s32[]{:S(2)}) async-start(), calls=%async_computation.23 | async-start | bytes 8650752 | tf_op jit(solution)/shard_map/reduce_scatter | solution.py:446
  1093.1 930.9 %reduce-scatter.14.cloned.1.call-start = ((), (), s32[]{:S(2)}) async-start(), calls=%async_computation.17 | async-start | bytes 12976128 | tf_op jit(solution)/shard_map/reduce_scatter | solution.py:438
  1109.6 1103.6 %reduce-scatter.24.cloned.1.call-start = ((), (), s32[]{:S(2)}) async-start(), calls=%async_computation.22 | async-start | bytes 17301504 | tf_op jit(solution)/shard_map/reduce_scatter | solution.py:445
  (76 other events, 1764.2 us)
Sparse Core Ops, SparseCore 0:
  10.9 55.6 all-gather.20
  69.5 71.6 all-gather.16
  143.9 38.0 all-gather.22
  360.4 61.3 all-gather.30
  424.5 58.4 all-gather.18
  485.8 52.7 all-gather.24
  541.4 77.2 all-gather.26
  621.6 60.5 all-gather.28
  709.5 57.6 all-gather.32
  770.4 84.6 reduce-scatter.11
  1070.7 128.3 reduce-scatter.27
  1201.8 132.3 reduce-scatter.21
  1341.1 119.7 reduce-scatter.19
  1463.6 111.5 reduce-scatter.15
  1581.3 132.5 reduce-scatter.17
  1716.7 127.3 reduce-scatter.25
  1851.6 172.2 reduce-scatter.13
  2026.7 186.5 reduce-scatter.23
where the time goes:
time: 2240 us; the launch traced here: 2220 us
  waiting for transfers between devices  1240 us (55%)
  matrix products  327 us (15%)
  local copies, waits for them, and re-layouts  250 us (11%)
  blocking collectives  219 us (10%)
  other arithmetic  157 us (7%)
    reduce_scatter x1, waiting for transfers between devices, body(): lax.psum_scatter(gate_up_grad, ('seq', 'rep'), scatter_dimension=0, tiled...  189 us
    reduce_scatter x1, waiting for transfers between devices, body(): lax.psum_scatter(inner_grad, ('seq', 'rep'), scatter_dimension=0, tiled=T...  180 us
    reduce_scatter x1, waiting for transfers between devices, body(): lax.psum_scatter(mixer_out_grad, ('seq', 'rep'), scatter_dimension=0, til...  139 us
    reduce_scatter x1, waiting for transfers between devices, body(): lax.psum_scatter(attend_out_grad, ('seq', 'rep'), scatter_dimension=0, ti...  134 us
    reduce_scatter x1, waiting for transfers between devices, body(): lax.psum_scatter(down_grad, ('seq', 'rep'), scatter_dimension=0, tiled=True)  130 us
    unnamed x4, blocking collectives  128 us
    reduce_scatter x1, waiting for transfers between devices, body(): lax.psum_scatter(project_grad, ('seq', 'rep'), scatter_dimension=0, tiled...  127 us
    reduce_scatter x1, waiting for transfers between devices, body(): lax.psum_scatter(states_grad, ('seq', 'rep'), scatter_dimension=0, tiled=...  114 us
  transfers between devices with their start and end apart: 18, of which 13 were waited for; matrix products, arithmetic and copies ran while one was open for 31% of the time, Pallas kernels for 0%

commit v1 on v0

v1 whole, which is shorter than its diff:
```python
import math

import jax
import jax.numpy as jnp
from jax import lax
from jax.sharding import PartitionSpec as P

FF = 2048
HEADS = 8
KV_HEADS = 2
HEAD_DIM = 64
SSM_HEADS = 24
SSM_DIM = 64
STATE = 128
D_SSM = 1536


EPS = 1e-06
WIDE = 128
HIGH = lax.Precision.HIGHEST


def project(left, right):
    return jnp.dot(left, right, preferred_element_type=jnp.float32)


def project_back(left, right):
    return lax.dot_general(
        left, right, (((1,), (1,)), ((), ())), preferred_element_type=jnp.float32
    )


def outer_sum(left, right):
    return lax.dot_general(
        left, right, (((0,), (0,)), ((), ())), preferred_element_type=jnp.float32
    )


def norm_rows(values, gain):
    inverse = lax.rsqrt(jnp.mean(values * values, axis=-1, keepdims=True) + EPS)
    return (values * inverse * gain, inverse)


def norm_back(grad, values, inverse, gain):
    scaled = values * inverse
    gain_grad = jnp.sum(grad * scaled, axis=0)
    weighted = grad * gain
    return (
        inverse * (weighted - scaled * jnp.mean(weighted * scaled, axis=-1, keepdims=True)),
        gain_grad,
    )


def heads_first(values, kind=jnp.bfloat16):
    rows = values.shape[0]
    return values.astype(kind).reshape(rows, SSM_HEADS, SSM_DIM).transpose(1, 0, 2)


def rows_first(values):
    return values.transpose(1, 0, 2).reshape(values.shape[1], D_SSM)


def spread_heads(values):
    return jnp.repeat(values, SSM_DIM, axis=-1)


def sum_heads(values):
    return jnp.sum(values.reshape(values.shape[0], SSM_HEADS, SSM_DIM), axis=-1)


def running_sum(values, reverse=False):
    places = jnp.arange(values.shape[0])
    if reverse:
        lower = places[None, :] >= places[:, None]
    else:
        lower = places[None, :] <= places[:, None]
    return jnp.dot(lower.astype(jnp.float32), values, precision=HIGH)


def decay_grid(cumul, masked):
    columns = cumul.T
    spread = columns[:, :, None] - columns[:, None, :]
    return jnp.exp(jnp.minimum(spread, 0.0)) * masked[None]


def link_weights(decays, firsts, lasts, place):
    count = decays.shape[0]
    keeps = jnp.where(firsts[1:] == lasts[:-1], 1.0, 0.0)
    keeps = jnp.concatenate([jnp.zeros_like(keeps[:1]), keeps])
    steps = decays * keeps[:, None]
    index = jnp.arange(count)
    source, middle = index[:, None, None], index[None, :, None]
    ahead = (source < middle) & (middle < place)
    ahead_product = jnp.prod(jnp.where(ahead, steps[None], 1.0), axis=1)
    own_keep = jnp.sum(jnp.where(index == place, keeps, 0.0))
    entry_weight = jnp.where((index < place)[:, None], ahead_product, 0.0) * own_keep
    behind = (place < middle) & (middle < source)
    behind_product = jnp.prod(jnp.where(behind, steps[None], 1.0), axis=1)
    exit_weight = jnp.where((index > place)[:, None], behind_product, 0.0) * keeps[:, None]
    return entry_weight, exit_weight


def weigh_states(weights, gathered):
    states = gathered.astype(jnp.float32).reshape(-1, SSM_HEADS, SSM_DIM, STATE)
    return jnp.sum(weights[:, :, None, None] * states, axis=0).reshape(D_SSM, STATE)


def visible(seg_float, seg_piece, query_pos, start, span):
    key_pos = start + jnp.arange(span)
    same = seg_float[:, None] == seg_piece.astype(jnp.float32)[None, :]
    causal = key_pos[None, :] <= query_pos[:, None]
    return (same & causal)[:, None, None, :]


def body(
    tokens,
    cotangent,
    segment_ids,
    input_gain,
    ssm_input,
    state_proj,
    step_proj,
    ssm_output,
    qkv_proj,
    attn_output,
    ffn_gain,
    gate_up,
    down_proj,
    head_params,
):
    rows = tokens.shape[1]
    width = HEADS * HEAD_DIM
    kv_width = KV_HEADS * HEAD_DIM
    group = HEADS // KV_HEADS
    scale = HEAD_DIM ** (-0.5)
    shard_rows = ssm_input.shape[0]
    padding = jnp.zeros((shard_rows, WIDE - SSM_HEADS - 2), jnp.bfloat16)
    first_full = lax.all_gather(
        jnp.concatenate(
            [
                ssm_input,
                qkv_proj,
                state_proj,
                step_proj,
                input_gain[:, None],
                ffn_gain[:, None],
                padding,
            ],
            axis=1,
        ),
        ("seq", "rep"),
        axis=0,
        tiled=True,
    )
    second_full = lax.all_gather(
        jnp.concatenate([ssm_output, attn_output, gate_up, down_proj], axis=1),
        ("seq", "rep"),
        axis=0,
        tiled=True,
    )
    qkv_at = 2 * D_SSM
    states_at = qkv_at + width + 2 * kv_width
    step_at = states_at + 2 * STATE
    gate_at = D_SSM + width
    down_at = gate_at + 2 * FF
    gain_first = first_full[:, step_at + SSM_HEADS]
    gain_second = first_full[:, step_at + SSM_HEADS + 1]
    out_full = second_full[:, :gate_at]
    gate_full = second_full[:, gate_at:down_at]
    down_full = second_full[:, down_at:]
    resident = tokens[0].astype(jnp.float32)
    segments = segment_ids[0]
    live = jnp.where(segments >= 0, 1.0, 0.0)[:, None]
    first_gain = gain_first.astype(jnp.float32)
    normed_float, inverse_one = norm_rows(resident, first_gain)
    normed = normed_float.astype(jnp.bfloat16)
    entered = project(normed, first_full)
    inner = entered[:, :qkv_at].astype(jnp.bfloat16)
    projected = entered[:, qkv_at:states_at].astype(jnp.bfloat16)
    states = entered[:, states_at:step_at].astype(jnp.bfloat16)
    step_raw = entered[:, step_at : step_at + SSM_HEADS]
    queries = projected[:, :width].reshape(rows, KV_HEADS, group, HEAD_DIM)
    key_vals = projected[:, width:]
    seg_float = segments.astype(jnp.float32)
    kv_wire = jnp.concatenate(
        [
            key_vals,
            segments.astype(jnp.bfloat16)[:, None],
            jnp.zeros((rows, WIDE - 1), jnp.bfloat16),
        ],
        axis=1,
    )
    kv_gathered = lax.all_gather(kv_wire, "seq", axis=0, tiled=True)
    kv_all = kv_gathered[:, : 2 * kv_width]
    seg_all = kv_gathered[:, 2 * kv_width]

    signal_low = inner[:, D_SSM:]
    signal = signal_low.astype(jnp.float32)
    gate_float = inner[:, :D_SSM].astype(jnp.float32)
    entry_map, read_map = states[:, :STATE], states[:, STATE:]
    earlier = jnp.concatenate([segments[:1], segments[:-1]])
    restarts = jnp.where(segments != earlier, 1.0, 0.0)
    shifted = step_raw + head_params[1]
    step_size = jax.nn.softplus(shifted)
    log_decay = -step_size * jnp.exp(head_params[0])
    cumul = running_sum(log_decay)
    counter = running_sum(restarts[:, None])[:, 0]
    places = jnp.arange(rows)
    joined = (counter[:, None] == counter[None, :]) & (places[None, :] <= places[:, None])
    joined = jnp.where(joined, 1.0, 0.0)
    crossing = project_back(read_map, entry_map) * joined
    reach = jnp.where((counter == 0)[:, None], jnp.exp(cumul), 0.0)
    closing = jnp.where((counter == counter[-1])[:, None], jnp.exp(cumul[-1][None, :] - cumul), 0.0)
    closing_step = spread_heads(closing * step_size)
    closed = (signal * closing_step).astype(jnp.bfloat16)
    ending = outer_sum(closed, entry_map)
    decay = reach[-1]
    decay_high = decay.astype(jnp.bfloat16)
    decay_low = (decay - decay_high.astype(jnp.float32)).astype(jnp.bfloat16)
    edges = jnp.stack([segments[0], segments[-1]]).astype(jnp.bfloat16)
    notes = jnp.concatenate(
        [decay_high, decay_low, edges, jnp.zeros((16 * STATE - 2 * SSM_HEADS - 2,), jnp.bfloat16)]
    ).reshape(16, STATE)
    state_wire = jnp.concatenate([ending.astype(jnp.bfloat16), notes], axis=0)
    state_gathered = lax.all_gather(state_wire, "seq", axis=0)
    noted = state_gathered[:, D_SSM].astype(jnp.float32)
    place = lax.axis_index("seq")
    entry_weight, exit_weight = link_weights(
        noted[:, :SSM_HEADS] + noted[:, SSM_HEADS : 2 * SSM_HEADS],
        noted[:, 2 * SSM_HEADS],
        noted[:, 2 * SSM_HEADS + 1],
        place,
    )
    signal_heads = heads_first(signal_low)
    mixing = decay_grid(cumul, crossing) * step_size.T[:, None, :]
    mixing_low = mixing.astype(jnp.bfloat16)
    within = jnp.einsum(
        "hts,hsp->htp", mixing_low, signal_heads, preferred_element_type=jnp.float32
    )
    skip = spread_heads(head_params[2])[None]
    reach_wide = spread_heads(reach)
    mixed_zero = rows_first(within) + skip * signal
    entry = weigh_states(entry_weight, state_gathered[:, :D_SSM])
    entry_low = entry.astype(jnp.bfloat16)
    read_entry = project_back(read_map, entry_low)
    mixed = mixed_zero + reach_wide * read_entry
    sig_gate = jax.nn.sigmoid(gate_float)
    gated = (mixed * gate_float * sig_gate).astype(jnp.bfloat16)
    row_start = lax.axis_index("seq") * rows
    query_pos = row_start + jnp.arange(rows)
    row_last = row_start + rows - 1
    span = kv_all.shape[0]

    keys_all = kv_all[:, :kv_width].reshape(span, KV_HEADS, HEAD_DIM)
    values_all = kv_all[:, kv_width:].reshape(span, KV_HEADS, HEAD_DIM)
    scores_all = (
        jnp.einsum("tgjd,sgd->tgjs", queries, keys_all, preferred_element_type=jnp.float32) * scale
    )
    allowed_all = visible(seg_float, seg_all, query_pos, 0, span)
    masked = jnp.where(allowed_all, scores_all, -1e30)
    top = jnp.max(masked, axis=-1)
    weights_all = jnp.where(allowed_all, jnp.exp(masked - top[..., None]), 0.0)
    total = jnp.sum(weights_all, axis=-1)
    weighted = jnp.einsum(
        "tgjs,sgd->tgjd",
        weights_all.astype(jnp.bfloat16),
        values_all,
        preferred_element_type=jnp.float32,
    )
    attended_float = weighted / total[..., None]
    log_total = top + jnp.log(total)
    attended = attended_float.reshape(rows, width).astype(jnp.bfloat16)
    mixed_low = jnp.concatenate([gated, attended], axis=1)
    mixed_out = project_back(mixed_low, out_full)
    hidden = resident + live * mixed_out
    second_gain = gain_second.astype(jnp.float32)
    normed2_float, inverse_two = norm_rows(hidden, second_gain)
    normed2 = normed2_float.astype(jnp.bfloat16)
    gate_vals = project(normed2, gate_full)
    gate_part = gate_vals[:, :FF]
    up_part = gate_vals[:, FF:]
    sigma = jax.nn.sigmoid(gate_part)
    activated = (gate_part * sigma * up_part).astype(jnp.bfloat16)
    result = hidden + live * project_back(activated, down_full)
    layer_out = result.astype(jnp.bfloat16)[None]
    upstream = cotangent[0].astype(jnp.float32)
    ffn_wire = (live * upstream).astype(jnp.bfloat16)
    down_grad = outer_sum(ffn_wire, activated)
    activated_grad = project(ffn_wire, down_full)
    gate_grad = activated_grad * up_part * sigma * (1.0 + gate_part * (1.0 - sigma))
    up_grad = activated_grad * gate_part * sigma
    gate_up_wire = jnp.concatenate([gate_grad, up_grad], axis=1).astype(jnp.bfloat16)
    gate_up_grad = outer_sum(normed2, gate_up_wire)
    normed2_grad = project_back(gate_up_wire, gate_full)
    hidden_back, gain_two_grad = norm_back(normed2_grad, hidden, inverse_two, second_gain)
    hidden_grad = upstream + hidden_back
    mixed_wire = (live * hidden_grad).astype(jnp.bfloat16)
    out_proj_grad = outer_sum(mixed_wire, mixed_low)
    mixed_low_wire = project(mixed_wire, out_full).astype(jnp.bfloat16)
    gated_wire = mixed_low_wire[:, :D_SSM].astype(jnp.float32)
    attended_wire = mixed_low_wire[:, D_SSM:]
    mixed_grad = gated_wire * gate_float * sig_gate
    gate_float_grad = gated_wire * mixed * sig_gate * (1.0 + gate_float * (1.0 - sig_gate))
    mixed_grad_low = mixed_grad.astype(jnp.bfloat16)
    reached = (mixed_grad * reach_wide).astype(jnp.bfloat16)
    entry_grad = outer_sum(reached, read_map)
    grad_gathered = lax.all_gather(entry_grad.astype(jnp.bfloat16), "seq", axis=0)
    out_grad = attended_wire.reshape(rows, KV_HEADS, group, HEAD_DIM)
    out_grad_float = out_grad.astype(jnp.float32)
    delta = jnp.sum(out_grad_float * attended_float, axis=-1)
    group_rows = kv_all.shape[0]
    block = math.gcd(group_rows, 512)
    count = group_rows // block

    def key_block(query_sum, piece):
        kv_piece, seg_piece, start = piece

        def key_work(unused):
            keys = kv_piece[:, :kv_width].reshape(block, KV_HEADS, HEAD_DIM)
            values = kv_piece[:, kv_width:].reshape(block, KV_HEADS, HEAD_DIM)
            scores = (
                jnp.einsum("tgjd,sgd->tgjs", queries, keys, preferred_element_type=jnp.float32)
                * scale
            )
            allowed = visible(seg_float, seg_piece, query_pos, start, block)
            probability = jnp.where(
                allowed, jnp.exp(jnp.where(allowed, scores - log_total[..., None], -1e30)), 0.0
            )
            values_grad = jnp.einsum(
                "tgjs,tgjd->sgd",
                probability.astype(jnp.bfloat16),
                out_grad,
                preferred_element_type=jnp.float32,
            )
            prob_grad = jnp.einsum(
                "tgjd,sgd->tgjs", out_grad, values, preferred_element_type=jnp.float32
            )
            score_wire = (probability * (prob_grad - delta[..., None])).astype(jnp.bfloat16)
            query_part = (
                jnp.einsum("tgjs,sgd->tgjd", score_wire, keys, preferred_element_type=jnp.float32)
                * scale
            )
            keys_grad = (
                jnp.einsum(
                    "tgjs,tgjd->sgd", score_wire, queries, preferred_element_type=jnp.float32
                )
                * scale
            )
            block_grad = jnp.concatenate(
                [keys_grad.reshape(block, kv_width), values_grad.reshape(block, kv_width)], axis=1
            )
            return (query_part, block_grad)

        def skip(unused):
            return (jnp.zeros_like(query_sum), jnp.zeros((block, 2 * kv_width), jnp.float32))

        query_part, block_grad = lax.cond(start <= row_last, key_work, skip, 0)
        return (query_sum + query_part, block_grad)

    starts = jnp.arange(count) * block
    query_grad, key_grads = lax.scan(
        key_block,
        jnp.zeros((rows, KV_HEADS, group, HEAD_DIM), jnp.float32),
        (kv_all.reshape(count, block, 2 * kv_width), seg_all.reshape(count, block), starts),
    )
    own_kv = lax.psum_scatter(
        key_grads.reshape(group_rows, 2 * kv_width).astype(jnp.bfloat16),
        "seq",
        scatter_dimension=0,
        tiled=True,
    ).astype(jnp.float32)
    early_grads = jnp.concatenate(
        [
            out_proj_grad.astype(jnp.bfloat16),
            gate_up_grad.astype(jnp.bfloat16),
            down_grad.astype(jnp.bfloat16),
        ],
        axis=1,
    )
    early_grads, own_kv, grad_gathered = lax.optimization_barrier(
        (early_grads, own_kv, grad_gathered)
    )
    early_owned = lax.psum_scatter(
        early_grads, ("seq", "rep"), scatter_dimension=0, tiled=True
    ).astype(jnp.float32)

    end_grad = weigh_states(exit_weight, grad_gathered)
    end_low = end_grad.astype(jnp.bfloat16)
    decay_grad = jnp.sum((end_grad * entry).reshape(SSM_HEADS, -1), axis=1)
    grad_heads = heads_first(mixed_grad_low)
    mixing_grad = jnp.einsum(
        "htp,hsp->hts", grad_heads, signal_heads, preferred_element_type=jnp.float32
    )
    signal_within = jnp.einsum(
        "hts,htp->hsp", mixing_low, grad_heads, preferred_element_type=jnp.float32
    )
    decay_part = decay_grid(cumul, joined)
    crossing_grad = jnp.sum(mixing_grad * decay_part * step_size.T[:, None, :], axis=0).astype(
        jnp.bfloat16
    )
    stepless = mixing_grad * decay_part * crossing[None]
    step_within = jnp.sum(stepless, axis=1).T
    row_within = jnp.sum(stepless * step_size.T[:, None, :], axis=2).T
    end_read = project_back(entry_map, end_low)
    signal_grad = rows_first(signal_within) + end_read * closing_step + skip * mixed_grad
    entry_map_grad = outer_sum(crossing_grad, read_map) + project(closed, end_low)
    read_map_grad = project(crossing_grad, entry_map) + project(reached, entry_low)
    reach_grad = sum_heads(mixed_grad * read_entry)
    closed_grad = sum_heads(end_read * signal)
    closing_part = closed_grad * step_size * closing
    cumul_grad = row_within - step_within * step_size + reach_grad * reach - closing_part
    last_grad = jnp.sum(closing_part, axis=0) + decay_grad * decay
    cumul_grad = cumul_grad + jnp.where((places == rows - 1)[:, None], last_grad[None], 0.0)
    log_grad = running_sum(cumul_grad, reverse=True)
    step_size_grad = step_within + closed_grad * closing - log_grad * jnp.exp(head_params[0])
    step_grad = step_size_grad * jax.nn.sigmoid(shifted)
    head_grad = jnp.stack(
        [
            jnp.sum(log_grad * log_decay, axis=0),
            jnp.sum(step_grad, axis=0),
            jnp.sum(sum_heads(mixed_grad * signal), axis=0),
        ]
    )
    first_wire = jnp.concatenate(
        [
            gate_float_grad.astype(jnp.bfloat16),
            signal_grad.astype(jnp.bfloat16),
            query_grad.reshape(rows, width).astype(jnp.bfloat16),
            own_kv.astype(jnp.bfloat16),
            entry_map_grad.astype(jnp.bfloat16),
            read_map_grad.astype(jnp.bfloat16),
            step_grad.astype(jnp.bfloat16),
            jnp.zeros((rows, WIDE - SSM_HEADS), jnp.bfloat16),
        ],
        axis=1,
    )
    late_owned = lax.psum_scatter(
        outer_sum(normed, first_wire).astype(jnp.bfloat16),
        ("seq", "rep"),
        scatter_dimension=0,
        tiled=True,
    ).astype(jnp.float32)
    normed_grad = project_back(first_wire, first_full)
    resident_back, gain_one_grad = norm_back(normed_grad, resident, inverse_one, first_gain)
    input_grad = (hidden_grad + resident_back).astype(jnp.bfloat16)[None]
    model = resident.shape[1]
    small_sum = lax.psum(
        jnp.concatenate([gain_one_grad, gain_two_grad, head_grad.reshape(-1)]), ("seq", "rep")
    )
    mine = (place * lax.axis_size("rep") + lax.axis_index("rep")) * shard_rows
    return (
        layer_out,
        input_grad,
        lax.dynamic_slice_in_dim(small_sum, mine, shard_rows),
        late_owned[:, :qkv_at],
        late_owned[:, states_at:step_at],
        late_owned[:, step_at : step_at + SSM_HEADS],
        early_owned[:, :D_SSM],
        late_owned[:, qkv_at:states_at],
        early_owned[:, D_SSM:gate_at],
        lax.dynamic_slice_in_dim(small_sum, model + mine, shard_rows),
        early_owned[:, gate_at:down_at],
        early_owned[:, down_at:],
        small_sum[2 * model :].reshape(head_grad.shape),
    )


def solution(mesh):
    placed = (
        P("rep", "seq", None),
        P("rep", "seq", None),
        P("rep", "seq"),
        P(("seq", "rep")),
        P(("seq", "rep"), None),
        P(("seq", "rep"), None),
        P(("seq", "rep"), None),
        P(("seq", "rep"), None),
        P(("seq", "rep"), None),
        P(("seq", "rep"), None),
        P(("seq", "rep")),
        P(("seq", "rep"), None),
        P(("seq", "rep"), None),
        P(),
    )
    return jax.shard_map(
        body,
        mesh=mesh,
        in_specs=placed,
        out_specs=(
            P("rep", "seq", None),
            P("rep", "seq", None),
            P(("seq", "rep")),
            P(("seq", "rep"), None),
            P(("seq", "rep"), None),
            P(("seq", "rep"), None),
            P(("seq", "rep"), None),
            P(("seq", "rep"), None),
            P(("seq", "rep"), None),
            P(("seq", "rep")),
            P(("seq", "rep"), None),
            P(("seq", "rep"), None),
            P(),
        ),
        check_vma=False,
    )
```

time: 2240 us -> 886 us (0.40)
  waiting for transfers between devices: 1240 us -> 589 us
  matrix products: 327 us -> 105 us
  blocking collectives: 219 us -> 39 us
  local copies, waits for them, and re-layouts: 250 us -> 79.5 us
  other arithmetic: 157 us -> 46.5 us
    reduce_scatter x7 -> x2, waiting for transfers between devices: 1010 us -> 259 us  [the longest x1 183 us: body(): lax.psum_scatter(early_grads, ('seq', 'rep'), scatter_dimension=0, tiled=...]
    dot_general x103 -> x10, matrix products: 235 us -> 27.2 us  [the longest x1 5.63 us: body(): jnp.einsum('htp,hsp->hts', grad_heads, signal_heads, preferred_element_ty...]
    unnamed x4 -> x0, blocking collectives: 128 us -> none
    dynamic_update_slice x168 -> x0, local copies, waits for them, and re-layouts: 102 us -> none  [local_ssm(): (ending, decay), (parts, reach) = lax.scan(advance, start, pieces)]
    all_gather x3 -> x0, blocking collectives: 91.4 us -> none  [the longest x1 39.7 us: body(): lax.all_gather(shards[2], ('seq', 'rep'), axis=0, tiled=True)]
    all_gather x9 -> x5, waiting for transfers between devices: 220 us -> 290 us  [the longest x1 105 us: body(): lax.all_gather(jnp.concatenate([ssm_output, attn_output, gate_up, down_pr...]
    reduce_scatter x1, waiting for transfers between devices: 0.02 us -> 39.9 us  [body(): lax.psum_scatter(key_grads.reshape(group_rows, 2 * kv_width).astype(jnp.b...]
    dynamic_update_slice x32 -> x0, other arithmetic: 39.3 us -> none  [local_ssm(): (ending, decay), (parts, reach) = lax.scan(advance, start, pieces)]
  transfers between devices with their start and end apart: 18 -> 8, of which waited for: 13 -> 8; matrix products, arithmetic and copies ran while one was open for 31% -> 15% of each run, Pallas kernels for 0% -> 0%
where the time goes in v1:
time: 886 us; the launch traced here: 879 us
  waiting for transfers between devices  589 us (66%)
  matrix products  105 us (12%)
  local copies, waits for them, and re-layouts  79.5 us (9%)
  other arithmetic  46.5 us (5%)
  blocking collectives  39 us (4%)
  between operations  16 us (2%)
    reduce_scatter x1, waiting for transfers between devices, body(): lax.psum_scatter(early_grads, ('seq', 'rep'), scatter_dimension=0, tiled=...  183 us
    all_gather x1, waiting for transfers between devices, body(): lax.all_gather(jnp.concatenate([ssm_output, attn_output, gate_up, down_pr...  105 us
    all_gather x1, waiting for transfers between devices, body(): lax.all_gather(jnp.concatenate([ssm_input, qkv_proj, state_proj, step_pro...  78 us
    reduce_scatter x1, waiting for transfers between devices, body(): lax.psum_scatter(outer_sum(normed, first_wire).astype(jnp.bfloat16), ('se...  75.4 us
    all_gather x1, waiting for transfers between devices, body(): lax.all_gather(entry_grad.astype(jnp.bfloat16), 'seq', axis=0)  63.1 us
    reduce_scatter x1, waiting for transfers between devices, body(): lax.psum_scatter(key_grads.reshape(group_rows, 2 * kv_width).astype(jnp.b...  39.9 us
    psum x1, blocking collectives, body(): lax.psum(jnp.concatenate([gain_one_grad, gain_two_grad, head_grad.reshape...  39 us
    all_gather x1, waiting for transfers between devices, body(): state_gathered = lax.all_gather(state_wire, 'seq', axis=0)  35.4 us
  transfers between devices with their start and end apart: 8, of which 8 were waited for; matrix products, arithmetic and copies ran while one was open for 15% of the time, Pallas kernels for 0%

profile of v1, /device:TPU:9, one launch (start us, length us, event | category | flops | bytes accessed | tf_op | source)
XLA Modules:
  0.0 879.3 jit_solution(16257407021150439954)
XLA Ops:
  13.5 78.0 %all-gather.8.cloned.1.call-done = bf16[1024,4224]{1,0:T(8,128)(2,1)} async-done(((bf16[32,4224]{1,0:T(8,128)(2,1)}), bf16[1024,4224]{1,0:T(8,128)(2,1)}) %all-gather.8.cloned.1.call-update) | async-done | bytes 8650768 | tf_op jit(solution)/shard_map/all_gather | solution.py:138
  92.9 8.2 fusion.163
  136.1 7.9 all-gather.10.cloned.1.call-done
  163.9 4.6 fusion.164
  169.3 35.4 %all-gather.14.cloned.1.call-done = bf16[12416,128]{1,0:T(8,128)(2,1)} async-done(((bf16[1552,128]{1,0:T(8,128)(2,1)}), bf16[12416,128]{1,0:T(8,128)(2,1)}) %all-gather.14.cloned.1.call-update) | async-done | bytes 3178512 | tf_op jit(solution)/shard_map/all_gather | solution.py:225
  212.5 4.6 fusion.48
  217.0 105.2 %all-gather.12.cloned.1.call-done = bf16[1024,8192]{1,0:T(8,128)(2,1)} async-done(((bf16[32,8192]{1,0:T(8,128)(2,1)}), bf16[1024,8192]{1,0:T(8,128)(2,1)}) %all-gather.12.cloned.1.call-update) | async-done | bytes 16777232 | tf_op jit(solution)/shard_map/all_gather | solution.py:155
  326.3 6.2 fusion.24
  343.8 26.5 %while.13 = (s32[]{:T(128)}, f32[256,2,4,64]{0,3,2,1:T(8,128)S(1)}, bf16[4,512,256]{1,2,0:T(8,128)(2,1)}, s32[4]{0:T(128)S(1)}, s32[]{:T(128)}, /*index=5*/f32[2...) while((s32[]{:T(128)}, f32[256,2,4,64]{0,3,2,1:T(8,128)S(1)}, ...), condition=%wide.region_13.14_spmd.clone, body=%wide.region_10.13_spmd.clone.sunk | while | flops 685114624 | bytes 25205552 | solution.py:361
  345.6 8.6 conditional.3
  356.3 8.6 conditional.3
  388.6 5.6 multiply_reduce_fusion
  403.2 6.7 pad_maximum_fusion
  409.9 39.9 %reduce-scatter.4.cloned.1.call-done = bf16[256,256]{1,0:T(8,128)(2,1)} async-done(((bf16[2048,256]{1,0:T(8,128)(2,1)}), bf16[256,256]{1,0:T(8,128)(2,1)}) %reduce-scatter.4.cloned.1.call-update) | async-done | bytes 131088 | tf_op jit(solution)/shard_map/reduce_scatter | solution.py:366
  449.8 63.1 %all-gather.16.cloned.1.call-done = bf16[12288,128]{1,0:T(8,128)(2,1)} async-done(((bf16[1536,128]{1,0:T(8,128)(2,1)}), bf16[12288,128]{1,0:T(8,128)(2,1)}) %all-gather.16.cloned.1.call-update) | async-done | bytes 3145744 | tf_op jit(solution)/shard_map/all_gather | solution.py:307
  513.0 4.5 multiply_reduce_fusion.2
  519.4 5.6 convert_multiply_fusion.4
  534.6 4.7 concatenate.54
  539.3 7.5 convolution_convert_fusion
  548.1 4.6 fusion.72
  553.0 7.1 fusion.87
  560.1 39.0 %psum.7 = f32[2120]{0:T(1024)S(1)} all-reduce(f32[2120]{0:T(1024)S(1)} %pad_maximum_fusion.9), channel_id=1, replica_groups=mesh['seq'=8,'rep'=4] {'seq','rep'}, use_global_device_ids=true, to_apply=%region_31.32 | all-reduce | flops 2120 | bytes 16960 | tf_op jit(solution)/shard_map/psum | solution.py:447
  601.5 75.4 %reduce-scatter.6.cloned.1.call-done = bf16[32,4224]{1,0:T(8,128)(2,1)} async-done(((bf16[1024,4224]{1,0:T(8,128)(2,1)}), bf16[32,4224]{1,0:T(8,128)(2,1)}) %reduce-scatter.6.cloned.1.call-update) | async-done | bytes 270352 | tf_op jit(solution)/shard_map/reduce_scatter | solution.py:437
  682.7 183.1 %reduce-scatter.8.cloned.1.call-done = bf16[32,8192]{1,0:T(8,128)(2,1)} async-done(((bf16[1024,8192]{1,0:T(8,128)(2,1)}), bf16[32,8192]{1,0:T(8,128)(2,1)}) %reduce-scatter.8.cloned.1.call-update) | async-done | bytes 524304 | tf_op jit(solution)/shard_map/reduce_scatter | solution.py:383
  (329 shorter events, 163.1 us)
Async XLA Ops:
  7.2 84.3 %all-gather.8.cloned.1.call-start = ((), (), s32[]{:S(2)}) async-start(), calls=%async_computation.3 | async-start | bytes 8921088 | tf_op jit(solution)/shard_map/all_gather | solution.py:138
  11.3 132.7 %all-gather.10.cloned.1.call-start = ((), (), s32[]{:S(2)}) async-start(), calls=%async_computation.4 | async-start | bytes 1769472 | tf_op jit(solution)/shard_map/all_gather | solution.py:193
  13.5 87.7 %copy-start.30 = (f32[256]{0:T(256)}, f32[256]{0:T(256)S(1)}, u32[]{:S(2)}) copy-start(f32[256]{0:T(256)S(1)} %add_rsqrt_fusion.1) | copy-start | bytes 3076
  92.9 13.6 %copy-start.47 = (f32[3,24]{1,0:T(4,128)S(1)}, f32[3,24]{1,0:T(4,128)}, u32[]{:S(2)}) copy-start(f32[3,24]{1,0:T(4,128)} %param.31) | copy-start | bytes 868
  101.1 110.4 %copy-start = (bf16[256,4224]{1,0:T(8,128)(2,1)}, bf16[256,4224]{1,0:T(8,128)(2,1)S(1)}, u32[]{:S(2)}) copy-start(bf16[256,4224]{1,0:T(8,128)(2,1)S(1)} %get-tuple-element.479) | copy-start | bytes 6488068
  102.0 102.7 %all-gather.14.cloned.1.call-start = ((), (), s32[]{:S(2)}) async-start(), calls=%async_computation.9 | async-start | bytes 3575808 | tf_op jit(solution)/shard_map/all_gather | solution.py:225
  104.0 235.7 %copy-start.33 = (f32[256]{0:T(256)}, f32[256]{0:T(256)S(1)}, u32[]{:S(2)}) copy-start(f32[256]{0:T(256)S(1)} %get-tuple-element.469) | copy-start | bytes 3076
  106.5 22.2 %copy-start.44 = (pred[256]{0:T(512)(128)(4,1)}, pred[256]{0:T(512)(128)(4,1)S(1)}, u32[]{:S(2)}) copy-start(pred[256]{0:T(512)(128)(4,1)S(1)} %get-tuple-element.471) | copy-start | bytes 772
  106.6 22.2 %copy-start.45 = (f32[24]{0:T(128)}, f32[24]{0:T(128)S(1)}, u32[]{:S(2)}) copy-start(f32[24]{0:T(128)S(1)} %get-tuple-element.467) | copy-start | bytes 292
  107.8 280.8 %copy-start.27 = (f32[256,24]{0,1:T(8,128)}, f32[256,24]{0,1:T(8,128)S(1)}, u32[]{:S(2)}) copy-start(f32[256,24]{0,1:T(8,128)S(1)} %fusion.95) | copy-start | bytes 73732
  108.8 23.0 %copy-start.26 = (f32[256,24]{0,1:T(8,128)}, f32[256,24]{0,1:T(8,128)S(1)}, u32[]{:S(2)}) copy-start(f32[256,24]{0,1:T(8,128)S(1)} %get-tuple-element.463) | copy-start | bytes 73732
  116.7 205.5 %all-gather.12.cloned.1.call-start = ((), (), s32[]{:S(2)}) async-start(), calls=%async_computation.5 | async-start | bytes 17301504 | tf_op jit(solution)/shard_map/all_gather | solution.py:155
  117.6 332.2 %reduce-scatter.4.cloned.1.call-start = ((), (), s32[]{:S(2)}) async-start(), calls=%async_computation.6 | async-start | bytes 1179648 | tf_op jit(solution)/shard_map/reduce_scatter | solution.py:366
  163.8 42.6 %copy-start.48 = (pred[8,8]{1,0:T(8,128)(4,1)S(1)}, pred[8,8]{1,0:T(8,128)(4,1)}, u32[]{:S(2)}) copy-start(pred[8,8]{1,0:T(8,128)(4,1)} %fusion.134) | copy-start | bytes 196
  163.8 42.6 %copy-start.49 = (pred[8,8]{1,0:T(8,128)(4,1)S(1)}, pred[8,8]{1,0:T(8,128)(4,1)}, u32[]{:S(2)}) copy-start(pred[8,8]{1,0:T(8,128)(4,1)} %fusion.135) | copy-start | bytes 196
  163.8 42.7 %copy-start.52 = (pred[8]{0:T(512)(128)(4,1)S(1)}, pred[8]{0:T(512)(128)(4,1)}, u32[]{:S(2)}) copy-start(pred[8]{0:T(512)(128)(4,1)} %copy-done.51) | copy-start | bytes 28
  212.5 109.7 %copy-start.2 = (bf16[1,256,1024]{2,1,0:T(8,128)(2,1)S(1)}, bf16[1,256,1024]{2,1,0:T(8,128)(2,1)}, u32[]{:S(2)}) copy-start(bf16[1,256,1024]{2,1,0:T(8,128)(2,1)} %param.18) | copy-start | bytes 1572868
  322.2 10.3 %slice-start.1 = ((s8[16777216]{0:T(1024)(128)(4,1)}), s8[4194304]{0:T(1024)(128)(4,1)S(1)}, s32[]{:S(2)}) async-start(s8[16777216]{0:T(1024)(128)(4,1)} %bitcast.268), calls=%async_computation.12 | async-start | bytes 8388608
  326.3 13.0 %copy-start.6 = (f32[256,1024]{1,0:T(8,128)}, f32[256,1024]{1,0:T(8,128)S(1)}, u32[]{:S(2)}) copy-start(f32[256,1024]{1,0:T(8,128)S(1)} %get-tuple-element.487) | copy-start | bytes 3145732
  326.3 13.0 %copy-start.38 = (f32[256]{0:T(256)}, f32[256]{0:T(256)S(1)}, u32[]{:S(2)}) copy-start(f32[256]{0:T(256)S(1)} %add_rsqrt_fusion) | copy-start | bytes 3076
  372.6 140.4 %all-gather.16.cloned.1.call-start = ((), (), s32[]{:S(2)}) async-start(), calls=%async_computation.10 | async-start | bytes 3538944 | tf_op jit(solution)/shard_map/all_gather | solution.py:307
  378.0 298.9 %reduce-scatter.6.cloned.1.call-start = ((), (), s32[]{:S(2)}) async-start(), calls=%async_computation.7 | async-start | bytes 8921088 | tf_op jit(solution)/shard_map/reduce_scatter | solution.py:437
  409.9 107.9 %copy-start.1 = (f32[256,1536]{1,0:T(8,128)S(1)}, f32[256,1536]{1,0:T(8,128)}, u32[]{:S(2)}) copy-start(f32[256,1536]{1,0:T(8,128)} %copy.284) | copy-start | bytes 4718596
  546.9 319.0 %reduce-scatter.8.cloned.1.call-start = ((), (), s32[]{:S(2)}) async-start(), calls=%async_computation.8 | async-start | bytes 17301504 | tf_op jit(solution)/shard_map/reduce_scatter | solution.py:383
  (47 other events, 249.7 us)
Sparse Core Ops, SparseCore 0:
  11.5 79.9 all-gather.7
  102.1 41.8 all-gather.9
  146.2 58.5 all-gather.13
  208.0 114.0 all-gather.11
  372.7 77.0 reduce-scatter.3
  452.7 60.2 all-gather.15
  547.0 129.8 reduce-scatter.5
  679.3 186.5 reduce-scatter.7

commit v2 on v1

--- a/solution.py
+++ b/solution.py
@@ -83,26 +83,65 @@
     return jnp.exp(jnp.minimum(spread, 0.0)) * masked[None]
 
 
-def link_weights(decays, firsts, lasts, place):
-    count = decays.shape[0]
+def swap(values, bit):
+    count = lax.axis_size("seq")
+    return lax.ppermute(values, "seq", [(i, i ^ bit) for i in range(count)])
+
+
+def bits_of(count):
+    return [1 << at for at in range(count.bit_length() - 1)]
+
+
+def gather_blocks(block, place):
+    blocks = block[None]
+    for bit in reversed(bits_of(lax.axis_size("seq"))):
+        arrived = swap(blocks, bit)
+        late = (place & bit) != 0
+        pair = jnp.stack(
+            [jnp.where(late, arrived, blocks), jnp.where(late, blocks, arrived)], axis=1
+        )
+        blocks = pair.reshape(-1, *block.shape)
+    return blocks
+
+
+def scatter_blocks(blocks, place):
+    for bit in bits_of(lax.axis_size("seq")):
+        pair = blocks.reshape(-1, 2, *blocks.shape[1:])
+        late = (place & bit) != 0
+        own = jnp.where(late, pair[:, 1], pair[:, 0])
+        other = jnp.where(late, pair[:, 0], pair[:, 1])
+        blocks = own + swap(other.astype(jnp.bfloat16), bit).astype(jnp.float32)
+    return blocks[0]
+
+
+def link_steps(decays, firsts, lasts):
     keeps = jnp.where(firsts[1:] == lasts[:-1], 1.0, 0.0)
     keeps = jnp.concatenate([jnp.zeros_like(keeps[:1]), keeps])
-    steps = decays * keeps[:, None]
-    index = jnp.arange(count)
-    source, middle = index[:, None, None], index[None, :, None]
-    ahead = (source < middle) & (middle < place)
-    ahead_product = jnp.prod(jnp.where(ahead, steps[None], 1.0), axis=1)
-    own_keep = jnp.sum(jnp.where(index == place, keeps, 0.0))
-    entry_weight = jnp.where((index < place)[:, None], ahead_product, 0.0) * own_keep
-    behind = (place < middle) & (middle < source)
-    behind_product = jnp.prod(jnp.where(behind, steps[None], 1.0), axis=1)
-    exit_weight = jnp.where((index > place)[:, None], behind_product, 0.0) * keeps[:, None]
-    return entry_weight, exit_weight
-
-
-def weigh_states(weights, gathered):
-    states = gathered.astype(jnp.float32).reshape(-1, SSM_HEADS, SSM_DIM, STATE)
-    return jnp.sum(weights[:, :, None, None] * states, axis=0).reshape(D_SSM, STATE)
+    return keeps, decays * keeps[:, None]
+
+
+def span_product(steps, start, stop):
+    index = jnp.arange(steps.shape[0])[:, None]
+    inside = (index >= start) & (index < stop)
+    return jnp.repeat(jnp.prod(jnp.where(inside, steps, 1.0), axis=0), SSM_DIM)[:, None]
+
+
+def link_scan(value, steps, place, reverse):
+    total, entering = value, jnp.zeros_like(value)
+    for bit in bits_of(lax.axis_size("seq")):
+        arrived = swap(total.astype(jnp.bfloat16), bit).astype(jnp.float32)
+        base = place - place % bit
+        far = ((place & bit) == 0) if reverse else ((place & bit) != 0)
+        own_span = span_product(steps, base, base + bit)
+        other = base ^ bit
+        other_span = span_product(steps, other, other + bit)
+        if reverse:
+            reaching = span_product(steps, place + 1, base + bit)
+        else:
+            reaching = span_product(steps, base, place)
+        entering = entering + jnp.where(far, reaching, 0.0) * arrived
+        total = jnp.where(far, total + own_span * arrived, arrived + other_span * total)
+    return entering
 
 
 def visible(seg_float, seg_piece, query_pos, start, span):
@@ -152,12 +191,10 @@
         axis=0,
         tiled=True,
     )
-    second_full = lax.all_gather(
-        jnp.concatenate([ssm_output, attn_output, gate_up, down_proj], axis=1),
-        ("seq", "rep"),
-        axis=0,
-        tiled=True,
-    )
+    second_shard, first_full = lax.optimization_barrier(
+        (jnp.concatenate([ssm_output, attn_output, gate_up, down_proj], axis=1), first_full)
+    )
+    second_full = lax.all_gather(second_shard, ("seq", "rep"), axis=0, tiled=True)
     qkv_at = 2 * D_SSM
     states_at = qkv_at + width + 2 * kv_width
     step_at = states_at + 2 * STATE
@@ -182,18 +219,6 @@
     queries = projected[:, :width].reshape(rows, KV_HEADS, group, HEAD_DIM)
     key_vals = projected[:, width:]
     seg_float = segments.astype(jnp.float32)
-    kv_wire = jnp.concatenate(
-        [
-            key_vals,
-            segments.astype(jnp.bfloat16)[:, None],
-            jnp.zeros((rows, WIDE - 1), jnp.bfloat16),
-        ],
-        axis=1,
-    )
-    kv_gathered = lax.all_gather(kv_wire, "seq", axis=0, tiled=True)
-    kv_all = kv_gathered[:, : 2 * kv_width]
-    seg_all = kv_gathered[:, 2 * kv_width]
-
     signal_low = inner[:, D_SSM:]
     signal = signal_low.astype(jnp.float32)
     gate_float = inner[:, :D_SSM].astype(jnp.float32)
@@ -210,27 +235,35 @@
     joined = jnp.where(joined, 1.0, 0.0)
     crossing = project_back(read_map, entry_map) * joined
     reach = jnp.where((counter == 0)[:, None], jnp.exp(cumul), 0.0)
+    decay = reach[-1]
+    decay_high = decay.astype(jnp.bfloat16)
+    decay_low = (decay - decay_high.astype(jnp.float32)).astype(jnp.bfloat16)
+    note_size = 2 * SSM_HEADS + rows
+    note_rows = 16 * (-(-note_size // (16 * 2 * kv_width)))
+    notes = jnp.concatenate(
+        [
+            decay_high,
+            decay_low,
+            segments.astype(jnp.bfloat16),
+            jnp.zeros((note_rows * 2 * kv_width - note_size,), jnp.bfloat16),
+        ]
+    ).reshape(note_rows, 2 * kv_width)
+    place = lax.axis_index("seq")
+    kv_blocks = gather_blocks(jnp.concatenate([key_vals, notes], axis=0), place)
+    group_rows = kv_blocks.shape[0] * rows
+    kv_all = kv_blocks[:, :rows].reshape(group_rows, 2 * kv_width)
+    noted = kv_blocks[:, rows:].reshape(kv_blocks.shape[0], -1)
+    seg_blocks = noted[:, 2 * SSM_HEADS : note_size].astype(jnp.float32)
+    seg_all = seg_blocks.reshape(group_rows)
+    decays = noted[:, : 2 * SSM_HEADS].astype(jnp.float32)
+    keeps, steps = link_steps(
+        decays[:, :SSM_HEADS] + decays[:, SSM_HEADS:], seg_blocks[:, 0], seg_blocks[:, -1]
+    )
+    own_keep = jnp.sum(jnp.where(jnp.arange(keeps.shape[0]) == place, keeps, 0.0))
     closing = jnp.where((counter == counter[-1])[:, None], jnp.exp(cumul[-1][None, :] - cumul), 0.0)
     closing_step = spread_heads(closing * step_size)
     closed = (signal * closing_step).astype(jnp.bfloat16)
     ending = outer_sum(closed, entry_map)
-    decay = reach[-1]
-    decay_high = decay.astype(jnp.bfloat16)
-    decay_low = (decay - decay_high.astype(jnp.float32)).astype(jnp.bfloat16)
-    edges = jnp.stack([segments[0], segments[-1]]).astype(jnp.bfloat16)
-    notes = jnp.concatenate(
-        [decay_high, decay_low, edges, jnp.zeros((16 * STATE - 2 * SSM_HEADS - 2,), jnp.bfloat16)]
-    ).reshape(16, STATE)
-    state_wire = jnp.concatenate([ending.astype(jnp.bfloat16), notes], axis=0)
-    state_gathered = lax.all_gather(state_wire, "seq", axis=0)
-    noted = state_gathered[:, D_SSM].astype(jnp.float32)
-    place = lax.axis_index("seq")
-    entry_weight, exit_weight = link_weights(
-        noted[:, :SSM_HEADS] + noted[:, SSM_HEADS : 2 * SSM_HEADS],
-        noted[:, 2 * SSM_HEADS],
-        noted[:, 2 * SSM_HEADS + 1],
-        place,
-    )
     signal_heads = heads_first(signal_low)
     mixing = decay_grid(cumul, crossing) * step_size.T[:, None, :]
     mixing_low = mixing.astype(jnp.bfloat16)
@@ -240,7 +273,7 @@
     skip = spread_heads(head_params[2])[None]
     reach_wide = spread_heads(reach)
     mixed_zero = rows_first(within) + skip * signal
-    entry = weigh_states(entry_weight, state_gathered[:, :D_SSM])
+    entry = own_keep * link_scan(ending, steps, place, False)
     entry_low = entry.astype(jnp.bfloat16)
     read_entry = project_back(read_map, entry_low)
     mixed = mixed_zero + reach_wide * read_entry
@@ -304,11 +337,10 @@
     mixed_grad_low = mixed_grad.astype(jnp.bfloat16)
     reached = (mixed_grad * reach_wide).astype(jnp.bfloat16)
     entry_grad = outer_sum(reached, read_map)
-    grad_gathered = lax.all_gather(entry_grad.astype(jnp.bfloat16), "seq", axis=0)
+    end_grad = link_scan(own_keep * entry_grad, steps, place, True)
     out_grad = attended_wire.reshape(rows, KV_HEADS, group, HEAD_DIM)
     out_grad_float = out_grad.astype(jnp.float32)
     delta = jnp.sum(out_grad_float * attended_float, axis=-1)
-    group_rows = kv_all.shape[0]
     block = math.gcd(group_rows, 512)
     count = group_rows // block
 
@@ -363,12 +395,7 @@
         jnp.zeros((rows, KV_HEADS, group, HEAD_DIM), jnp.float32),
         (kv_all.reshape(count, block, 2 * kv_width), seg_all.reshape(count, block), starts),
     )
-    own_kv = lax.psum_scatter(
-        key_grads.reshape(group_rows, 2 * kv_width).astype(jnp.bfloat16),
-        "seq",
-        scatter_dimension=0,
-        tiled=True,
-    ).astype(jnp.float32)
+    own_kv = scatter_blocks(key_grads.reshape(-1, rows, 2 * kv_width), place)
     early_grads = jnp.concatenate(
         [
             out_proj_grad.astype(jnp.bfloat16),
@@ -377,14 +404,10 @@
         ],
         axis=1,
     )
-    early_grads, own_kv, grad_gathered = lax.optimization_barrier(
-        (early_grads, own_kv, grad_gathered)
-    )
     early_owned = lax.psum_scatter(
         early_grads, ("seq", "rep"), scatter_dimension=0, tiled=True
-    ).astype(jnp.float32)
-
-    end_grad = weigh_states(exit_weight, grad_gathered)
+    )
+
     end_low = end_grad.astype(jnp.bfloat16)
     decay_grad = jnp.sum((end_grad * entry).reshape(SSM_HEADS, -1), axis=1)
     grad_heads = heads_first(mixed_grad_low)
@@ -434,12 +457,13 @@
         ],
         axis=1,
     )
+    late_grads, early_owned = lax.optimization_barrier(
+        (outer_sum(normed, first_wire).astype(jnp.bfloat16), early_owned)
+    )
     late_owned = lax.psum_scatter(
-        outer_sum(normed, first_wire).astype(jnp.bfloat16),
-        ("seq", "rep"),
-        scatter_dimension=0,
-        tiled=True,
+        late_grads, ("seq", "rep"), scatter_dimension=0, tiled=True
     ).astype(jnp.float32)
+    early_owned = early_owned.astype(jnp.float32)
     normed_grad = project_back(first_wire, first_full)
     resident_back, gain_one_grad = norm_back(normed_grad, resident, inverse_one, first_gain)
     input_grad = (hidden_grad + resident_back).astype(jnp.bfloat16)[None]

time: 886 us -> 627 us (0.71)
  waiting for transfers between devices: 589 us -> 252 us
  starting transfers between devices: 0.54 us -> 46 us
  other arithmetic: 46.5 us -> 60.7 us
  matrix products: 105 us -> 115 us
    all_gather x4 -> x1, waiting for transfers between devices: 212 us -> 0.02 us  [body(): lax.all_gather(second_shard, ('seq', 'rep'), axis=0, tiled=True)]
    reduce_scatter x1, waiting for transfers between devices: 183 us -> 0.02 us  [body(): lax.psum_scatter(early_grads, ('seq', 'rep'), scatter_dimension=0, tiled=...]
    ppermute x0 -> x12, waiting for transfers between devices: none -> 94.4 us  [swap(): return lax.ppermute(values, 'seq', [(i, i ^ bit) for i in range(count)])]
    ppermute x0 -> x12, starting transfers between devices: none -> 45.8 us  [swap(): return lax.ppermute(values, 'seq', [(i, i ^ bit) for i in range(count)])]
    reduce_scatter x2 -> x1, waiting for transfers between devices: 115 us -> 79.1 us  [body(): lax.psum_scatter(late_grads, ('seq', 'rep'), scatter_dimension=0, tiled=T...]
  transfers between devices with their start and end apart: 8 -> 16, of which waited for: 8 -> 8; matrix products, arithmetic and copies ran while one was open for 15% -> 35% of each run, Pallas kernels for 0% -> 0%
where the time goes in v2:
time: 627 us; the launch traced here: 616 us
  waiting for transfers between devices  252 us (40%)
  matrix products  115 us (18%)
  local copies, waits for them, and re-layouts  84.9 us (14%)
  other arithmetic  60.7 us (10%)
  starting transfers between devices  46 us (7%)
  blocking collectives  39.6 us (6%)
  between operations  15.3 us (2%)
    ppermute x12, waiting for transfers between devices, swap(): return lax.ppermute(values, 'seq', [(i, i ^ bit) for i in range(count)])  94.4 us
    reduce_scatter x1, waiting for transfers between devices, body(): lax.psum_scatter(late_grads, ('seq', 'rep'), scatter_dimension=0, tiled=T...  79.1 us
    all_gather x1, waiting for transfers between devices, body(): lax.all_gather(jnp.concatenate([ssm_input, qkv_proj, state_proj, step_pro...  78.2 us
    ppermute x12, starting transfers between devices, swap(): return lax.ppermute(values, 'seq', [(i, i ^ bit) for i in range(count)])  45.8 us
    psum x1, blocking collectives, body(): lax.psum(jnp.concatenate([gain_one_grad, gain_two_grad, head_grad.reshape...  39.6 us
    dot_general x7, matrix products, project_back(): lax.dot_general(left, right, (((1,), (1,)), ((), ())), preferred_element_...  33.5 us
    dot_general x7, matrix products, project(): return jnp.dot(left, right, preferred_element_type=jnp.float32)  27.1 us
    dot_general x7, matrix products, outer_sum(): lax.dot_general(left, right, (((0,), (0,)), ((), ())), preferred_element_...  18.3 us
  transfers between devices with their start and end apart: 16, of which 8 were waited for; matrix products, arithmetic and copies ran while one was open for 35% of the time, Pallas kernels for 0%

profile of v2, /device:TPU:9, one launch (start us, length us, event | category | flops | bytes accessed | tf_op | source)
XLA Modules:
  0.0 616.0 jit_solution(78630213585478460)
XLA Ops:
  13.3 78.2 %all-gather.3.cloned.1.call-done = bf16[1024,4224]{1,0:T(8,128)(2,1)} async-done(((bf16[32,4224]{1,0:T(8,128)(2,1)}), bf16[1024,4224]{1,0:T(8,128)(2,1)}) %all-gather.3.cloned.1.call-update) | async-done | bytes 8650768 | tf_op jit(solution)/shard_map/all_gather | solution.py:177
  98.8 6.2 %fusion.189 = (bf16[256,4224]{1,0:T(8,128)(2,1)S(1)}, f32[256,4224]{1,0:T(8,128)S(1)}) fusion(bf16[1024,4224]{1,0:T(8,128)(2,1)} %all-gather.3.cloned.1.call-done, bf16[1,256,1024]{2,1,0:T(8,128)(2,1)S(1)} %copy-done.4, f32[1024]{0:T(1024)S(1)} %get-tuple-element.408, f32[256]{0:T(256)S(1)} %add_rsqrt_fusion.1), kind=kOutput, calls=%fused_computation.315 | convolution fusion | flops 2216722432 | bytes 15668224 | tf_op jit(solution)/shard_map/dot_general | solution.py:24
  107.7 10.3 %collective-permute-done = bf16[1,272,256]{2,1,0:T(8,128)(2,1)} collective-permute-done((bf16[1,272,256]{2,1,0:T(8,128)(2,1)S(1)}, bf16[1,272,256]{2,1,0:T(8,128)(2,1)}, u32[]{:S(2)}, u32[]{:S(2)}) %collective-permute-start) | collective-permute-done | bytes 139296 | tf_op jit(solution)/shard_map/ppermute | solution.py:88
  181.5 15.5 %collective-permute-done.4 = bf16[1536,128]{1,0:T(8,128)(2,1)} collective-permute-done((bf16[1536,128]{1,0:T(8,128)(2,1)}, bf16[1536,128]{1,0:T(8,128)(2,1)}, u32[]{:S(2)}, u32[]{:S(2)}) %collective-permute-start.4) | collective-permute-done | bytes 393248 | tf_op jit(solution)/shard_map/ppermute | solution.py:88
  200.1 6.3 %collective-permute-start.5 = (bf16[1536,128]{1,0:T(8,128)(2,1)}, bf16[1536,128]{1,0:T(8,128)(2,1)}, u32[]{:S(2)}, u32[]{:S(2)}) collective-permute-start(bf16[1536,128]{1,0:T(8,128)(2,1)} %fusion.99), channel_id=1, source_target_pairs={{0,16},{4,20},{8,24},{12,28},{16,0},{20,4},{24,8},{28,12},{1,17},{... | collective-permute-start | bytes 1179656 | tf_op jit(solution)/shard_map/ppermute | solution.py:88
  206.8 24.8 %collective-permute-done.5 = bf16[1536,128]{1,0:T(8,128)(2,1)} collective-permute-done((bf16[1536,128]{1,0:T(8,128)(2,1)}, bf16[1536,128]{1,0:T(8,128)(2,1)}, u32[]{:S(2)}, u32[]{:S(2)}) %collective-permute-start.5) | collective-permute-done | bytes 393248 | tf_op jit(solution)/shard_map/ppermute | solution.py:88
  231.6 6.0 fusion.48
  241.6 6.2 %fusion.24 = f32[256,4096]{1,0:T(8,128)S(1)} fusion(bf16[1024,8192]{1,0:T(8,128)(2,1)} %all-gather.5.cloned.1.call-done, f32[256,1024]{1,0:T(8,128)S(1)} %get-tuple-element.507, f32[1024]{0:T(1024)S(1)} %get-tuple-element.407, f32[256]{0:T(256)S(1)} %add_rsqrt_fusion), kind=kOutput, calls=%fused_computation.38 | convolution fusion | flops 2148270080 | bytes 13636608 | tf_op jit(solution)/shard_map/dot_general | solution.py:24
  254.6 6.5 %multiply_reduce_fusion.3 = (f32[1024]{0:T(1024)}, f32[256]{0:T(256)S(1)}, f32[256,1024]{1,0:T(8,128)S(1)}) fusion(f32[256,1024]{1,0:T(8,128)S(1)} %get-tuple-element.507, f32[256]{0:T(256)S(1)} %add_rsqrt_fusion, f32[1024]{0:T(1024)S(1)} %get-tuple-element.407, bf16[1024,8192]{1,0:T(8,128)(2,1)} %all-gather.5.cloned.1.call-done, ...), kind=kOutput, calls=%fused_computation.136 | convolution fusion | flops 2153249536 | bytes 12593152 | tf_op jit(solution)/shard_map/dot_general | solution.py:28
  265.1 6.9 %pad_maximum_fusion = bf16[1024,8192]{1,0:T(8,128)(2,1)} fusion(bf16[1024,2048]{1,0:T(8,128)(2,1)S(1)} %convolution_convert_fusion.2, bf16[1024,4096]{1,0:T(8,128)(2,1)S(1)} %convolution_convert_fusion.1, bf16[1024,2048]{1,0:T(8,128)(2,1)S(1)} %convolution_convert_fusion.3), kind=kLoop, calls=%fused_computation.26 | loop fusion | flops 50331648 | bytes 33554432 | tf_op jit(solution)/shard_map/concatenate | solution.py:399
  300.9 28.9 %while.13 = (s32[]{:T(128)}, f32[256,2,4,64]{0,3,2,1:T(8,128)S(1)}, f32[4,512,256]{2,1,0:T(8,128)}, s32[4]{0:T(128)S(1)}, s32[]{:T(128)}, /*index=5*/f32[256]{0:...) while((s32[]{:T(128)}, f32[256,2,4,64]{0,3,2,1:T(8,128)S(1)}, ...), condition=%wide.region_20.21_spmd.clone, body=%wide.region_17.20_spmd.clone.sunk | while | flops 684655360 | bytes 27598768 | solution.py:393
  302.2 9.3 %conditional.3 = (f32[256,2,4,64]{0,3,2,1:T(8,128)S(1)}, f32[1,512,256]{1,2,0:T(8,128)S(1)}) conditional(s32[]{:T(128)} %convert_element_type.646, () %tuple.118, (f32[256]{0:T(256)S(1)}, f32[4,512]{1,0:T(4,128)}, s32[]{:T(128)}, s32[]{:T(128)}, s32[]{:T(128)}, /*index=5*/bf16[4,512,256]{1,2,0:T(8,128)(2,1)}, ...), branch_computations={%region_18.18_spmd, %region_19.19_spmd} | conditional | flops 684393216 | bytes 23926844 | solution.py:389
  314.0 9.3 %conditional.3 = (f32[256,2,4,64]{0,3,2,1:T(8,128)S(1)}, f32[1,512,256]{1,2,0:T(8,128)S(1)}) conditional(s32[]{:T(128)} %convert_element_type.646, () %tuple.118, (f32[256]{0:T(256)S(1)}, f32[4,512]{1,0:T(4,128)}, s32[]{:T(128)}, s32[]{:T(128)}, s32[]{:T(128)}, /*index=5*/bf16[4,512,256]{1,2,0:T(8,128)(2,1)}, ...), branch_computations={%region_18.18_spmd, %region_19.19_spmd} | conditional | flops 684393216 | bytes 23926844 | solution.py:389
  336.6 5.3 multiply_reduce_fusion
  354.5 10.7 %collective-permute-done.7 = bf16[1536,128]{1,0:T(8,128)(2,1)S(1)} collective-permute-done((bf16[1536,128]{1,0:T(8,128)(2,1)S(1)}, bf16[1536,128]{1,0:T(8,128)(2,1)S(1)}, u32[]{:S(2)}, u32[]{:S(2)}) %collective-permute-start.7) | collective-permute-done | bytes 393248 | tf_op jit(solution)/shard_map/ppermute | solution.py:88
  366.4 23.0 %collective-permute-start.8 = (bf16[1536,128]{1,0:T(8,128)(2,1)S(1)}, bf16[1536,128]{1,0:T(8,128)(2,1)S(1)}, u32[]{:S(2)}, u32[]{:S(2)}) collective-permute-start(bf16[1536,128]{1,0:T(8,128)(2,1)S(1)} %fusion.106), channel_id=1, source_target_pairs={{0,16},{4,20},{8,24},{12,28},{16,0},{20,4},{24,8},{28,12},{1,17},{... | collective-permute-start | bytes 1179656 | tf_op jit(solution)/shard_map/ppermute | solution.py:88
  389.5 6.8 %collective-permute-start.11 = (bf16[1,256,256]{2,1,0:T(8,128)(2,1)S(1)}, bf16[1,256,256]{2,1,0:T(8,128)(2,1)S(1)}, u32[]{:S(2)}, u32[]{:S(2)}) collective-permute-start(bf16[1,256,256]{2,1,0:T(8,128)(2,1)S(1)} %fusion.128), channel_id=1, source_target_pairs={{0,16},{4,20},{8,24},{12,28},{16,0},{20,4},{24,8},{28,12},{1,17},{... | collective-permute-start | bytes 393224 | tf_op jit(solution)/shard_map/ppermute | solution.py:88
  397.5 31.0 %collective-permute-done.11 = bf16[1,256,256]{2,1,0:T(8,128)(2,1)S(1)} collective-permute-done((bf16[1,256,256]{2,1,0:T(8,128)(2,1)S(1)}, bf16[1,256,256]{2,1,0:T(8,128)(2,1)S(1)}, u32[]{:S(2)}, u32[]{:S(2)}) %collective-permute-start.11) | collective-permute-done | bytes 131104 | tf_op jit(solution)/shard_map/ppermute | solution.py:88
  429.2 5.8 convert_multiply_fusion.4
  446.5 5.0 multiply_reduce_fusion.6
  460.5 6.0 convolution_convert_fusion
  472.6 6.8 %fusion.87 = (f32[1024]{0:T(1024)S(1)}, f32[256]{0:T(256)S(1)}, f32[256,1024]{1,0:T(8,128)S(1)}) fusion(bf16[1,256,1024]{2,1,0:T(8,128)(2,1)S(1)} %copy-done.4, f32[256]{0:T(256)S(1)} %copy-done.50, f32[1024]{0:T(1024)S(1)} %copy-done.41, bf16[256,4224]{1,0:T(8,128)(2,1)} %copy-done.6, bf16[1024,4224]{1,0:T(8,128)(2,1)} %all-gather.3.cloned.1.call-done), kind=kOutput, calls=%fused_computation.132 | convolution fusion | flops 2216426240 | bytes 12396544 | tf_op jit(solution)/shard_map/dot_general | solution.py:28
  479.5 39.6 %psum.7 = f32[2120]{0:T(1024)S(1)} all-reduce(f32[2120]{0:T(1024)S(1)} %pad_maximum_fusion.10), channel_id=1, replica_groups=mesh['seq'=8,'rep'=4] {'seq','rep'}, use_global_device_ids=true, to_apply=%region_36.37 | all-reduce | flops 2120 | bytes 16960 | tf_op jit(solution)/shard_map/psum | solution.py:471
  524.4 79.1 %reduce-scatter.5.cloned.1.call-done = bf16[32,4224]{1,0:T(8,128)(2,1)} async-done(((bf16[1024,4224]{1,0:T(8,128)(2,1)}), bf16[32,4224]{1,0:T(8,128)(2,1)}) %reduce-scatter.5.cloned.1.call-update) | async-done | bytes 270352 | tf_op jit(solution)/shard_map/reduce_scatter | solution.py:463
  (457 shorter events, 211.9 us)
Async XLA Ops:
  7.2 84.4 %copy-start.65 = (s32[1,256]{1,0:T(1,128)S(1)}, s32[1,256]{1,0:T(1,128)}, u32[]{:S(2)}) copy-start(s32[1,256]{1,0:T(1,128)} %param.20) | copy-start | bytes 3076
  7.2 88.7 %copy-start.4 = (bf16[1,256,1024]{2,1,0:T(8,128)(2,1)S(1)}, bf16[1,256,1024]{2,1,0:T(8,128)(2,1)}, u32[]{:S(2)}) copy-start(bf16[1,256,1024]{2,1,0:T(8,128)(2,1)} %param.18) | copy-start | bytes 1572868
  7.2 90.1 %copy-start.88 = (f32[3,24]{1,0:T(4,128)S(1)}, f32[3,24]{1,0:T(4,128)}, u32[]{:S(2)}) copy-start(f32[3,24]{1,0:T(4,128)} %param.31) | copy-start | bytes 868
  7.2 84.3 %all-gather.3.cloned.1.call-start = ((), (), s32[]{:S(2)}) async-start(), calls=%async_computation.2 | async-start | bytes 8921088 | tf_op jit(solution)/shard_map/all_gather | solution.py:177
  11.4 226.2 %all-gather.5.cloned.1.call-start = ((), (), s32[]{:S(2)}) async-start(), calls=%async_computation.3 | async-start | bytes 17301504 | tf_op jit(solution)/shard_map/all_gather | solution.py:197
  91.6 374.9 %reduce-scatter.3.cloned.1.call-start = ((), (), s32[]{:S(2)}) async-start(), calls=%async_computation.4 | async-start | bytes 17301504 | tf_op jit(solution)/shard_map/reduce_scatter | solution.py:407
  105.0 189.2 %copy-start = (bf16[256,4224]{1,0:T(8,128)(2,1)}, bf16[256,4224]{1,0:T(8,128)(2,1)S(1)}, u32[]{:S(2)}) copy-start(bf16[256,4224]{1,0:T(8,128)(2,1)S(1)} %get-tuple-element.497) | copy-start | bytes 6488068
  106.0 12.0 %collective-permute-start = (bf16[1,272,256]{2,1,0:T(8,128)(2,1)S(1)}, bf16[1,272,256]{2,1,0:T(8,128)(2,1)}, u32[]{:S(2)}, u32[]{:S(2)}) collective-permute-start(bf16[1,272,256]{2,1,0:T(8,128)(2,1)S(1)} %maximum_bitcast_fusion.2), channel_id=1, source_target_pairs={{0,16},{4,20},{8,24},{12,28},{16,0},{20,4},{24,8},{28,12},{1,17},{... | collective-permute-start | bytes 417800 | tf_op jit(solution)/shard_map/ppermute | solution.py:88
  119.7 15.6 %collective-permute-start.1 = (bf16[2,272,256]{2,1,0:T(8,128)(2,1)}, bf16[2,272,256]{2,1,0:T(8,128)(2,1)}, u32[]{:S(2)}, u32[]{:S(2)}) collective-permute-start(bf16[2,272,256]{2,1,0:T(8,128)(2,1)} %maximum_bitcast_fusion.1), channel_id=1, source_target_pairs={{0,8},{4,12},{8,0},{12,4},{16,24},{20,28},{24,16},{28,20},{1,9},{5... | collective-permute-start | bytes 835592 | tf_op jit(solution)/shard_map/ppermute | solution.py:88
  137.3 17.2 %collective-permute-start.2 = (bf16[4,272,256]{2,1,0:T(8,128)(2,1)}, bf16[4,272,256]{2,1,0:T(8,128)(2,1)}, u32[]{:S(2)}, u32[]{:S(2)}) collective-permute-start(bf16[4,272,256]{2,1,0:T(8,128)(2,1)} %bitcast.45), channel_id=1, source_target_pairs={{0,4},{4,0},{8,12},{12,8},{16,20},{20,16},{24,28},{28,24},{1,5},{5... | collective-permute-start | bytes 1671176 | tf_op jit(solution)/shard_map/ppermute | solution.py:88
  152.3 11.8 %collective-permute-start.3 = (bf16[1536,128]{1,0:T(8,128)(2,1)}, bf16[1536,128]{1,0:T(8,128)(2,1)S(1)}, u32[]{:S(2)}, u32[]{:S(2)}) collective-permute-start(bf16[1536,128]{1,0:T(8,128)(2,1)} %get-tuple-element.503), channel_id=1, source_target_pairs={{0,4},{4,0},{8,12},{12,8},{16,20},{20,16},{24,28},{28,24},{1,5},{5... | collective-permute-start | bytes 1179656 | tf_op jit(solution)/shard_map/ppermute | solution.py:88
  166.6 30.4 %collective-permute-start.4 = (bf16[1536,128]{1,0:T(8,128)(2,1)}, bf16[1536,128]{1,0:T(8,128)(2,1)}, u32[]{:S(2)}, u32[]{:S(2)}) collective-permute-start(bf16[1536,128]{1,0:T(8,128)(2,1)} %fusion.170), channel_id=1, source_target_pairs={{0,8},{4,12},{8,0},{12,4},{16,24},{20,28},{24,16},{28,20},{1,9},{5... | collective-permute-start | bytes 1179656 | tf_op jit(solution)/shard_map/ppermute | solution.py:88
  200.1 31.5 %collective-permute-start.5 = (bf16[1536,128]{1,0:T(8,128)(2,1)}, bf16[1536,128]{1,0:T(8,128)(2,1)}, u32[]{:S(2)}, u32[]{:S(2)}) collective-permute-start(bf16[1536,128]{1,0:T(8,128)(2,1)} %fusion.99), channel_id=1, source_target_pairs={{0,16},{4,20},{8,24},{12,28},{16,0},{20,4},{24,8},{28,12},{1,17},{... | collective-permute-start | bytes 1179656 | tf_op jit(solution)/shard_map/ppermute | solution.py:88
  272.0 331.5 %reduce-scatter.5.cloned.1.call-start = ((), (), s32[]{:S(2)}) async-start(), calls=%async_computation.5 | async-start | bytes 8921088 | tf_op jit(solution)/shard_map/reduce_scatter | solution.py:463
  297.3 53.0 %collective-permute-start.6 = (bf16[1536,128]{1,0:T(8,128)(2,1)}, bf16[1536,128]{1,0:T(8,128)(2,1)S(1)}, u32[]{:S(2)}, u32[]{:S(2)}) collective-permute-start(bf16[1536,128]{1,0:T(8,128)(2,1)} %get-tuple-element.509), channel_id=1, source_target_pairs={{0,4},{4,0},{8,12},{12,8},{16,20},{20,16},{24,28},{28,24},{1,5},{5... | collective-permute-start | bytes 1179656 | tf_op jit(solution)/shard_map/ppermute | solution.py:88
  331.4 19.6 %collective-permute-start.9 = (bf16[4,256,256]{2,1,0:T(8,128)(2,1)S(1)}, bf16[4,256,256]{2,1,0:T(8,128)(2,1)}, u32[]{:S(2)}, u32[]{:S(2)}) collective-permute-start(bf16[4,256,256]{2,1,0:T(8,128)(2,1)S(1)} %fusion.107), channel_id=1, source_target_pairs={{0,4},{4,0},{8,12},{12,8},{16,20},{20,16},{24,28},{28,24},{1,5},{5... | collective-permute-start | bytes 1572872 | tf_op jit(solution)/shard_map/ppermute | solution.py:88
  350.8 14.4 %collective-permute-start.7 = (bf16[1536,128]{1,0:T(8,128)(2,1)S(1)}, bf16[1536,128]{1,0:T(8,128)(2,1)S(1)}, u32[]{:S(2)}, u32[]{:S(2)}) collective-permute-start(bf16[1536,128]{1,0:T(8,128)(2,1)S(1)} %fusion.169), channel_id=1, source_target_pairs={{0,8},{4,12},{8,0},{12,4},{16,24},{20,28},{24,16},{28,20},{1,9},{5... | collective-permute-start | bytes 1179656 | tf_op jit(solution)/shard_map/ppermute | solution.py:88
  351.0 78.1 %copy-start.99 = (f32[256,1536]{1,0:T(8,128)S(1)}, f32[256,1536]{1,0:T(8,128)}, u32[]{:S(2)}) copy-start(f32[256,1536]{1,0:T(8,128)} %get-tuple-element.505) | copy-start | bytes 4718596
  353.1 76.1 %copy-start.98 = (f32[256,1536]{1,0:T(8,128)S(1)}, f32[256,1536]{1,0:T(8,128)}, u32[]{:S(2)}) copy-start(f32[256,1536]{1,0:T(8,128)} %get-tuple-element.455) | copy-start | bytes 4718596
  353.2 36.3 %collective-permute-start.10 = (bf16[2,256,256]{2,1,0:T(8,128)(2,1)S(1)}, bf16[2,256,256]{2,1,0:T(8,128)(2,1)S(1)}, u32[]{:S(2)}, u32[]{:S(2)}) collective-permute-start(bf16[2,256,256]{2,1,0:T(8,128)(2,1)S(1)} %fusion.110), channel_id=1, source_target_pairs={{0,8},{4,12},{8,0},{12,4},{16,24},{20,28},{24,16},{28,20},{1,9},{5... | collective-permute-start | bytes 786440 | tf_op jit(solution)/shard_map/ppermute | solution.py:88
  365.2 64.0 %copy-start.14 = (bf16[1536,128]{1,0:T(8,128)(2,1)}, bf16[1536,128]{1,0:T(8,128)(2,1)S(1)}, u32[]{:S(2)}) copy-start(bf16[1536,128]{1,0:T(8,128)(2,1)S(1)} %collective-permute-done.7) | copy-start | bytes 1179652
  365.2 64.0 %copy-start.29 = (bf16[256,2048]{1,0:T(8,128)(2,1)S(1)}, bf16[256,2048]{1,0:T(8,128)(2,1)}, u32[]{:S(2)}) copy-start(bf16[256,2048]{1,0:T(8,128)(2,1)} %copy-done.28) | copy-start | bytes 3145732
  366.4 62.7 %collective-permute-start.8 = (bf16[1536,128]{1,0:T(8,128)(2,1)S(1)}, bf16[1536,128]{1,0:T(8,128)(2,1)S(1)}, u32[]{:S(2)}, u32[]{:S(2)}) collective-permute-start(bf16[1536,128]{1,0:T(8,128)(2,1)S(1)} %fusion.106), channel_id=1, source_target_pairs={{0,16},{4,20},{8,24},{12,28},{16,0},{20,4},{24,8},{28,12},{1,17},{... | collective-permute-start | bytes 1179656 | tf_op jit(solution)/shard_map/ppermute | solution.py:88
  389.5 38.9 %collective-permute-start.11 = (bf16[1,256,256]{2,1,0:T(8,128)(2,1)S(1)}, bf16[1,256,256]{2,1,0:T(8,128)(2,1)S(1)}, u32[]{:S(2)}, u32[]{:S(2)}) collective-permute-start(bf16[1,256,256]{2,1,0:T(8,128)(2,1)S(1)} %fusion.128), channel_id=1, source_target_pairs={{0,16},{4,20},{8,24},{12,28},{16,0},{20,4},{24,8},{28,12},{1,17},{... | collective-permute-start | bytes 393224 | tf_op jit(solution)/shard_map/ppermute | solution.py:88
  (96 other events, 1296.9 us)
Sparse Core Ops, SparseCore 0:
  11.5 79.9 all-gather.2
  95.0 136.3 all-gather.4
  272.1 192.5 reduce-scatter.2
  470.5 132.9 reduce-scatter.4
